TPU v7x, 32 devices: a whole 2x2x4 slice. The times are simulated.
32 devices in a mesh: dom: 8 (over y, x, core), blk: 4 (over z).
Axes of the slice: x: 2, y: 2, z: 4, core: 2. Of those that a mesh axis runs over, the one named last changes fastest.
Arguments:
- displacement: float32 [3, 64, 32, 128], P(None, 'dom', 'blk'), may hold values from -6 to 6
- velocity: float32 [3, 64, 32, 128], P(None, 'dom', 'blk'), may hold values from -6 to 6
- load: float32 [3, 64, 32, 128], P(None, 'dom', 'blk'), may hold values from -6 to 6
- density: float32 [64, 32, 128], P('dom', 'blk'), may hold values from 0.5 to 1.5
- block_class: int32 [8, 4, 16], P('dom', 'blk'), may hold values from 0 to 2
- host_element: int32 [4, 32768], P('blk', 'dom'), may hold values from 0 to 7038, as said below
- host_coords: float32 [3, 4, 32768], P(None, 'blk', 'dom'), may hold values from 0 to 1
- fibre_slot: int32 [128, 4, 128], P('dom', 'blk'), may hold values from 0 to 4095, as said below
- fibre_angles: float32 [2, 128, 4, 128], P(None, 'dom', 'blk'), may hold values from -3.140625 to 3.140625
- fibre_stiffness: float32 [128, 4], P('dom', 'blk'), may hold values from 0.5 to 4
Outputs:
- new_displacement: float32 [3, 64, 32, 128], P(None, 'dom', 'blk')
- new_velocity: float32 [3, 64, 32, 128], P(None, 'dom', 'blk')
Inputs may be any that keep to these rules, and one draw needn't show every extreme that they name: `host_element`: each entry is (i * 8 + j) * 128 + k with i < 7, j < 7, k < 127, a voxel element of the device's own block; a device's entries are laid out as 512 slots for each owner index along dom, in order. `fibre_slot`: the entries of one device are distinct; value // 512 is the dom index of the host device in the same blk column and value % 512 the slot among that host's 512 slots for this owner; on every device all 512 slots of one host are used.
All inputs are finite; a program needn't handle non-finite values.
Results may differ from a plain program's by a relative error of at most 0.0003.
Values sent between devices are 32-bit elements; how exact they have to be, the bound alone decides.
A program may use at most 64 MiB of HBM per device.

v0:
```python
import math

import jax
import jax.numpy as jnp
import numpy as np
from jax import lax
from jax.sharding import PartitionSpec as P

class_values = (1.0, 0.45, 0.12)
time_step = 0.25
damping = 0.5


def padded_2(block, sides, width):
    for axis, dim in sides:
        count = lax.axis_size(axis)
        forward = [(i, i + 1) for i in range(count - 1)]
        backward = [(target, source) for source, target in forward]
        low = lax.ppermute(
            lax.slice_in_dim(block, block.shape[dim] - width, None, axis=dim), axis, forward
        )
        high = lax.ppermute(lax.slice_in_dim(block, 0, width, axis=dim), axis, backward)
        block = jnp.concatenate([low, block, high], axis=dim)
    return block


def stiffness_table():
    poisson = 0.3
    lame = poisson / ((1 + poisson) * (1 - 2 * poisson))
    shear = 0.5 / (1 + poisson)
    elastic = np.zeros((6, 6))
    elastic[:3, :3] = lame
    for place in range(3):
        elastic[place, place] += 2 * shear
        elastic[place + 3, place + 3] = shear
    points = [0.5 - 0.5 / np.sqrt(3.0), 0.5 + 0.5 / np.sqrt(3.0)]
    table = np.zeros((24, 24))
    for gauss_r in points:
        for gauss_p in points:
            for gauss_q in points:
                strain = np.zeros((6, 24))
                for corner in range(8):
                    x_bit, y_bit, z_bit = (corner // 4, corner // 2 % 2, corner % 2)
                    along_r = gauss_r if x_bit else 1 - gauss_r
                    along_p = gauss_p if y_bit else 1 - gauss_p
                    along_q = gauss_q if z_bit else 1 - gauss_q
                    d_x = (2 * x_bit - 1) * along_p * along_q
                    d_y = along_r * (2 * y_bit - 1) * along_q
                    d_z = along_r * along_p * (2 * z_bit - 1)
                    column = 3 * corner
                    strain[0, column] = d_x
                    strain[1, column + 1] = d_y
                    strain[2, column + 2] = d_z
                    strain[3, column] = d_y
                    strain[3, column + 1] = d_x
                    strain[4, column + 1] = d_z
                    strain[4, column + 2] = d_y
                    strain[5, column] = d_z
                    strain[5, column + 2] = d_x
                table += 0.125 * strain.T @ elastic @ strain
    return table


def class_moduli(block_class):
    factor = jnp.zeros(block_class.shape, jnp.float32)
    for index, value in enumerate(class_values):
        factor = factor + jnp.where(block_class == index, jnp.float32(value), jnp.float32(0.0))
    bx, by, bz = block_class.shape
    wide = jnp.broadcast_to(factor[:, None, :, None, :, None], (bx, 8, by, 8, bz, 8))
    return wide.reshape(bx * 8, by * 8, bz * 8)


def lift_depth(local):
    return jnp.concatenate([local[..., 1:], jnp.zeros_like(local[..., :1])], axis=-1)


def element_forces(padded, moduli, density):
    width = padded.shape[1] - 2
    height = padded.shape[2] - 2
    depth = padded.shape[3]
    table = jnp.asarray(stiffness_table(), jnp.float32)
    element = jnp.zeros((24, width + 1, height + 1, depth), jnp.float32)
    for corner in range(8):
        x_bit, y_bit, z_bit = (corner // 4, corner // 2 % 2, corner % 2)
        local = padded[:, x_bit : x_bit + width + 1, y_bit : y_bit + height + 1, :]
        if z_bit:
            local = lift_depth(local)
        element = element + jnp.einsum(
            "ij,jxyz->ixyz",
            table[:, 3 * corner : 3 * corner + 3],
            local,
            precision=lax.Precision.HIGHEST,
        )
    element = element * moduli[None, : width + 1, : height + 1, :]
    weight = density[: width + 1, : height + 1, :]
    force = jnp.zeros((3, width, height, depth), jnp.float32)
    mass = jnp.zeros((width, height, depth), jnp.float32)
    for corner in range(8):
        x_bit, y_bit, z_bit = (corner // 4, corner // 2 % 2, corner % 2)
        piece = element[
            3 * corner : 3 * corner + 3,
            1 - x_bit : 1 - x_bit + width,
            1 - y_bit : 1 - y_bit + height,
            :,
        ]
        share = weight[1 - x_bit : 1 - x_bit + width, 1 - y_bit : 1 - y_bit + height, :]
        if z_bit:
            piece = jnp.pad(piece[..., :-1], ((0, 0), (0, 0), (0, 0), (1, 0)))
            share = jnp.pad(share[..., :-1], ((0, 0), (0, 0), (1, 0)))
        force = force + piece
        mass = mass + 0.125 * share
    return (force, mass)


def axis_weights(along, lowest, count):
    positions = lax.broadcasted_iota(jnp.int32, (count, along.shape[0]), 0)
    lower = jnp.where(positions == lowest[None], 1.0 - along[None], jnp.float32(0.0))
    upper = jnp.where(positions == lowest[None] + 1, along[None], jnp.float32(0.0))
    return lower + upper


def slot_weights(element, coords, width, height, depth):
    plane = height * depth
    along_x = element // plane
    along_y = element // depth % height
    along_z = element % depth
    weight_x = axis_weights(coords[0], along_x, width)
    weight_y = axis_weights(coords[1], along_y, height)
    weight_z = axis_weights(coords[2], along_z, depth)
    planar = (weight_x[:, None, :] * weight_y[None]).reshape(width * height, -1)
    return (planar, weight_z)


def interpolate(field, planar, weight_z):
    width, height, depth = (field.shape[1], field.shape[2], field.shape[3])
    partial_sums = jnp.dot(
        field.reshape(3 * width * height, depth), weight_z, precision=lax.Precision.HIGHEST
    )
    return jnp.sum(partial_sums.reshape(3, width * height, -1) * planar[None], axis=1)


def spread(force, planar, weight_z, width, height, depth):
    terms = (force[:, None, :] * planar[None]).reshape(3 * width * height, -1)
    summed = jnp.dot(terms, weight_z.T, precision=lax.Precision.HIGHEST)
    return summed.reshape(3, width, height, depth)


def pick_rows(places, wanted, span_rows):
    total = places.shape[1]
    groups = wanted.reshape(-1, span_rows)

    def pick_single(members):
        onehot = (
            members[:, None] == lax.broadcasted_iota(jnp.int32, (span_rows, total), 1)
        ).astype(jnp.float32)
        return jnp.dot(places, onehot.T, precision=lax.Precision.HIGHEST)

    picked = lax.map(pick_single, groups)
    return picked.transpose(1, 0, 2).reshape(3, -1)


def place_rows(values, wanted, total, span_rows):
    groups = wanted.reshape(-1, span_rows)
    pieces = values.reshape(3, -1, span_rows).transpose(1, 0, 2)

    def place_single(carry, item):
        members, stretch_values = item
        onehot = (
            members[:, None] == lax.broadcasted_iota(jnp.int32, (span_rows, total), 1)
        ).astype(jnp.float32)
        return (carry + jnp.dot(stretch_values, onehot, precision=lax.Precision.HIGHEST), None)

    result, _ = lax.scan(place_single, jnp.zeros((3, total), jnp.float32), (groups, pieces))
    return result


def fibre_forces(places, slots, angles, stiffness):
    total = places.shape[1]
    fibres, nodes = slots.shape
    wanted = slots.reshape(-1)
    span_rows = math.gcd(fibres * nodes, 512)
    node = pick_rows(places, wanted, span_rows).reshape(3, fibres, nodes)
    direction = jnp.stack(
        [
            jnp.cos(angles[0]) * jnp.cos(angles[1]),
            jnp.sin(angles[0]) * jnp.cos(angles[1]),
            jnp.sin(angles[1]),
        ]
    )
    ahead = jnp.concatenate([node[..., 1:], node[..., -1:]], axis=-1)
    strain = jnp.sum(direction * (ahead - node), axis=0)
    live = lax.broadcasted_iota(jnp.int32, strain.shape, 1) < strain.shape[1] - 1
    tension = jnp.where(live, stiffness * jnp.maximum(strain, 0.0), jnp.float32(0.0))
    pull = tension[None] * direction
    behind = jnp.concatenate([jnp.zeros_like(pull[..., :1]), pull[..., :-1]], axis=-1)
    return place_rows((pull - behind).reshape(3, -1), wanted, total, span_rows)


def shards(
    displacement,
    velocity,
    load,
    density,
    block_class,
    host_element,
    host_coords,
    fibre_slot,
    fibre_angles,
    fibre_stiffness,
):
    width, height, depth = (displacement.shape[1], displacement.shape[2], displacement.shape[3])
    parts = lax.axis_size("dom")
    moduli = class_moduli(block_class) * density * density
    element = host_element[0]
    coords = host_coords[:, 0]
    planar, weight_z = slot_weights(element, coords, width, height, depth)
    places = interpolate(displacement, planar, weight_z)
    received = lax.all_to_all(
        places.reshape(3, parts, -1), "dom", split_axis=1, concat_axis=1, tiled=True
    )
    pulls = fibre_forces(
        received.reshape(3, -1), fibre_slot[:, 0], fibre_angles[:, :, 0], fibre_stiffness
    )
    returned = lax.all_to_all(
        pulls.reshape(3, parts, -1), "dom", split_axis=1, concat_axis=1, tiled=True
    )
    fibre = spread(returned.reshape(3, -1), planar, weight_z, width, height, depth)
    fields = jnp.concatenate([displacement, moduli[None], density[None]], axis=0)
    padded = padded_2(fields, (("dom", 1), ("blk", 2)), 1)
    elastic, mass = element_forces(padded[:3], padded[3], padded[4])
    acceleration = (load - elastic + fibre) / mass[None] - damping * velocity
    new_velocity = velocity + time_step * acceleration
    new_displacement = displacement + time_step * new_velocity
    return (new_displacement, new_velocity)


def solution(mesh):
    return jax.shard_map(
        shards,
        mesh=mesh,
        in_specs=(
            P(None, "dom", "blk", None),
            P(None, "dom", "blk", None),
            P(None, "dom", "blk", None),
            P("dom", "blk", None),
            P("dom", "blk", None),
            P("blk", "dom"),
            P(None, "blk", "dom"),
            P("dom", "blk", None),
            P(None, "dom", "blk", None),
            P("dom", "blk"),
        ),
        out_specs=(P(None, "dom", "blk", None), P(None, "dom", "blk", None)),
        check_vma=False,
    )
```

profile of v0, /device:TPU:0, one launch (start us, length us, event | category | flops | bytes accessed | tf_op | source)
XLA Modules:
  0.0 80.4 jit_solution(5602749938861490695)
XLA Ops:
  0.6 0.7 fusion.53
  1.4 0.1 broadcast_in_dim.114
  1.5 1.0 %copy.44 = f32[3,8,8,128]{3,0,2,1:T(4,128)S(1)} copy(f32[3,8,8,128]{3,2,1,0:T(8,128)} %param.15) | data formatting | bytes 196608 | tf_op args[0]
  2.5 0.8 multiply_multiply_fusion
  3.2 0.7 pad_maximum_fusion.15
  4.0 1.3 %collective-permute-start.1 = (f32[5,1,8,128]{3,0,2,1:T(8,128)S(1)}, f32[5,1,8,128]{3,0,2,1:T(8,128)S(1)}, u32[]{:S(2)}, u32[]{:S(2)}) collective-permute-start(f32[5,1,8,128]{3,0,2,1:T(8,128)S(1)} %get-tuple-element.119), channel_id=1, source_target_pairs={{4,0},{8,4},{12,8},{16,12},{20,16},{24,20},{28,24},{5,1},{9,5},{13... | collective-permute-start | bytes 61448 | tf_op jit(solution)/shard_map/ppermute | solution.py:22
  5.3 3.0 %collective-permute-start = (f32[5,1,8,128]{3,0,2,1:T(8,128)S(1)}, f32[5,1,8,128]{3,0,2,1:T(8,128)S(1)}, u32[]{:S(2)}, u32[]{:S(2)}) collective-permute-start(f32[5,1,8,128]{3,0,2,1:T(8,128)S(1)} %get-tuple-element.118), channel_id=1, source_target_pairs={{0,4},{4,8},{8,12},{12,16},{16,20},{20,24},{24,28},{1,5},{5,9},{9,... | collective-permute-start | bytes 61448 | tf_op jit(solution)/shard_map/ppermute | solution.py:19
  8.3 0.8 fusion.65
  9.1 0.8 %broadcast_add_fusion.1 = (s32[1,4096]{1,0:T(1,128)S(1)}, s32[1,4096]{1,0:T(1,128)S(1)}, s32[1,4096]{1,0:T(1,128)S(1)}, s32[1,4096]{1,0:T(1,128)S(1)}, s32[1,4096]{1,0:T(1,128)S(1)}) fusion(s32[1,4096]{1,0:T(1,128)} %param.20), kind=kLoop, calls=%fused_computation.121 | loop fusion | flops 102400 | bytes 98304 | tf_op jit(solution)/shard_map/add | solution.py:118
  9.9 0.8 %broadcast_add_fusion = (s32[1,4096]{1,0:T(1,128)S(1)}, s32[1,4096]{1,0:T(1,128)S(1)}) fusion(s32[1,4096]{1,0:T(1,128)} %param.20, s32[1,4096]{1,0:T(1,128)S(1)} %get-tuple-element.134), kind=kLoop, calls=%fused_computation.120 | loop fusion | flops 98304 | bytes 65536 | tf_op jit(solution)/shard_map/add | solution.py:118
  10.9 0.1 fusion.27
  11.0 3.3 %fusion.9 = f32[4096,192]{0,1:T(8,128)S(1)} fusion(f32[192,128]{1,0:T(8,128)S(1)} %bitcast.118, f32[4096]{0:T(1024)S(1)} %bitcast.140, s32[4096]{0:T(1024)S(1)} %bitcast.146, f32[4096]{0:T(1024)S(1)} %broadcast_subtract_fusion.2, s32[4096]{0:T(1024)S(1)} %bitcast.148), kind=kOutput, calls=%fused_computation.18 | convolution fusion | flops 1210580992 | bytes 3309568 | tf_op jit(solution)/shard_map/dot_general | solution.py:136
  14.3 1.0 %multiply_reduce_fusion = f32[3,4096]{1,0:T(4,128)} fusion(f32[3,64,4096]{2,1,0:T(8,128)S(1)} %bitcast.107, f32[64,4096]{1,0:T(8,128)S(1)} %get-tuple-element.114), kind=kLoop, calls=%fused_computation.14 | loop fusion | flops 1560576 | bytes 4243456 | tf_op jit(solution)/shard_map/reduce_sum | solution.py:139
  15.4 5.8 %all-to-all-start = ((f32[3,8,512]{2,0,1:T(4,128)}), f32[3,8,512]{2,0,1:T(4,128)S(1)}, u32[]{:S(2)}, u32[]{:S(2)}) async-start(f32[3,8,512]{2,0,1:T(4,128)} %bitcast.39), calls=%async_computation | async-start | bytes 131072 | tf_op jit(solution)/shard_map/all_to_all | solution.py:218
  21.2 0.2 fusion.60
  21.6 0.5 broadcast.322
  22.1 0.6 reduce.8
  22.8 1.3 %collective-permute-start.3 = (f32[5,10,1,128]{3,0,2,1:T(8,128)S(1)}, f32[5,10,1,128]{3,0,2,1:T(8,128)S(1)}, u32[]{:S(2)}, u32[]{:S(2)}) collective-permute-start(f32[5,10,1,128]{3,0,2,1:T(8,128)S(1)} %get-tuple-element.117), channel_id=1, source_target_pairs={{1,0},{2,1},{3,2},{5,4},{6,5},{7,6},{9,8},{10,9},{11,10},{13,12},{... | collective-permute-start | bytes 76808 | tf_op jit(solution)/shard_map/ppermute | solution.py:22
  24.1 4.5 %collective-permute-start.2 = (f32[5,10,1,128]{3,0,2,1:T(8,128)S(1)}, f32[5,10,1,128]{3,0,2,1:T(8,128)S(1)}, u32[]{:S(2)}, u32[]{:S(2)}) collective-permute-start(f32[5,10,1,128]{3,0,2,1:T(8,128)S(1)} %get-tuple-element.116), channel_id=1, source_target_pairs={{0,1},{1,2},{2,3},{4,5},{5,6},{6,7},{8,9},{9,10},{10,11},{12,13},{... | collective-permute-start | bytes 76808 | tf_op jit(solution)/shard_map/ppermute | solution.py:19
  28.7 16.0 %while.21 = (s32[]{:T(128)}, f32[4,3,512]{2,0,1:T(4,128)S(1)}, s32[4,512]{1,0:T(4,128)S(1)}, f32[3,4096]{1,0:T(4,128)S(1)}, s32[]{:T(128)}, /*index=5*/s32[]{:T(128)}) while((s32[]{:T(128)}, f32[4,3,512]{2,0,1:T(4,128)S(1)}, s32[4,512]{1,0:T(4,128)S(1)}, f32[3,4096]{1,0:T(4,128)S(1)}, s32[]{:T(128)}, /*index=5*/s32[]{:T(128)}) %tuple.81), condition=%wide.region_2.3_spmd, body=%wide.region_1.2_spmd.sunk | while | flops 77594624 | bytes 86101 | solution.py:158
  28.7 3.9 %fusion.80 = f32[1,3,512]{2,1,0:T(4,128)S(1)} fusion(f32[3,4096]{1,0:T(4,128)S(1)} %get-tuple-element.204, s32[512]{0:T(512)S(1)} %bitcast.143), kind=kOutput, calls=%fused_computation.3.clone.1 | convolution fusion | flops 77594624 | bytes 57344 | tf_op jit(solution)/shard_map/while/body/eval_jaxpr/dot_general | solution.py:156
  32.7 3.9 %fusion.80 = f32[1,3,512]{2,1,0:T(4,128)S(1)} fusion(f32[3,4096]{1,0:T(4,128)S(1)} %get-tuple-element.204, s32[512]{0:T(512)S(1)} %bitcast.143), kind=kOutput, calls=%fused_computation.3.clone.1 | convolution fusion | flops 77594624 | bytes 57344 | tf_op jit(solution)/shard_map/while/body/eval_jaxpr/dot_general | solution.py:156
  36.7 3.9 %fusion.80 = f32[1,3,512]{2,1,0:T(4,128)S(1)} fusion(f32[3,4096]{1,0:T(4,128)S(1)} %get-tuple-element.204, s32[512]{0:T(512)S(1)} %bitcast.143), kind=kOutput, calls=%fused_computation.3.clone.1 | convolution fusion | flops 77594624 | bytes 57344 | tf_op jit(solution)/shard_map/while/body/eval_jaxpr/dot_general | solution.py:156
  40.7 3.9 %fusion.80 = f32[1,3,512]{2,1,0:T(4,128)S(1)} fusion(f32[3,4096]{1,0:T(4,128)S(1)} %get-tuple-element.204, s32[512]{0:T(512)S(1)} %bitcast.143), kind=kOutput, calls=%fused_computation.3.clone.1 | convolution fusion | flops 77594624 | bytes 57344 | tf_op jit(solution)/shard_map/while/body/eval_jaxpr/dot_general | solution.py:156
  45.1 0.1 pad_subtract_fusion
  45.2 16.3 %while.22 = (s32[]{:T(128)}, f32[3,4096]{1,0:T(4,128)}, f32[4,3,512]{2,0,1:T(4,128)S(1)}, s32[4,512]{1,0:T(4,128)S(1)}, s32[]{:T(128)}, /*index=5*/s32[]{:T(128)}) while((s32[]{:T(128)}, f32[3,4096]{1,0:T(4,128)}, f32[4,3,512]{2,0,1:T(4,128)S(1)}, s32[4,512]{1,0:T(4,128)S(1)}, s32[]{:T(128)}, /*index=5*/s32[]{:T(128)}) %tuple.80), condition=%wide.region_5.6_spmd.clone, body=%wide.region_4.5_spmd.clone.sunk | while | flops 77619200 | bytes 122975 | solution.py:173
  45.2 3.4 %fusion.81 = f32[3,4096]{1,0:T(4,128)} fusion(s32[512]{0:T(512)S(1)} %bitcast.142, f32[3,4096]{1,0:T(4,128)} %get-tuple-element.214, pred[]{:T(512)S(6)} %compare.30, f32[1,3,512]{2,0,1:T(1,128)S(1)} %constant_dynamic-slice_fusion.8), kind=kOutput, calls=%fused_computation.7.clone.1 | convolution fusion | flops 77619200 | bytes 106497 | tf_op jit(solution)/shard_map/while/body/eval_jaxpr/dot_general | solution.py:171
  48.7 4.3 %fusion.81 = f32[3,4096]{1,0:T(4,128)} fusion(s32[512]{0:T(512)S(1)} %bitcast.142, f32[3,4096]{1,0:T(4,128)} %get-tuple-element.214, pred[]{:T(512)S(6)} %compare.30, f32[1,3,512]{2,0,1:T(1,128)S(1)} %constant_dynamic-slice_fusion.8), kind=kOutput, calls=%fused_computation.7.clone.1 | convolution fusion | flops 77619200 | bytes 106497 | tf_op jit(solution)/shard_map/while/body/eval_jaxpr/dot_general | solution.py:171
  52.9 4.3 %fusion.81 = f32[3,4096]{1,0:T(4,128)} fusion(s32[512]{0:T(512)S(1)} %bitcast.142, f32[3,4096]{1,0:T(4,128)} %get-tuple-element.214, pred[]{:T(512)S(6)} %compare.30, f32[1,3,512]{2,0,1:T(1,128)S(1)} %constant_dynamic-slice_fusion.8), kind=kOutput, calls=%fused_computation.7.clone.1 | convolution fusion | flops 77619200 | bytes 106497 | tf_op jit(solution)/shard_map/while/body/eval_jaxpr/dot_general | solution.py:171
  57.2 4.3 %fusion.81 = f32[3,4096]{1,0:T(4,128)} fusion(s32[512]{0:T(512)S(1)} %bitcast.142, f32[3,4096]{1,0:T(4,128)} %get-tuple-element.214, pred[]{:T(512)S(6)} %compare.30, f32[1,3,512]{2,0,1:T(1,128)S(1)} %constant_dynamic-slice_fusion.8), kind=kOutput, calls=%fused_computation.7.clone.1 | convolution fusion | flops 77619200 | bytes 106497 | tf_op jit(solution)/shard_map/while/body/eval_jaxpr/dot_general | solution.py:171
  61.5 4.3 %all-to-all-start.1 = ((f32[3,8,512]{2,0,1:T(4,128)}), f32[3,8,512]{2,0,1:T(4,128)S(1)}, u32[]{:S(2)}, u32[]{:S(2)}) async-start(f32[3,8,512]{2,0,1:T(4,128)} %bitcast.46), calls=%async_computation.1 | async-start | bytes 131072 | tf_op jit(solution)/shard_map/all_to_all | solution.py:224
  65.8 0.2 pad_maximum_fusion.7
  66.0 0.1 maximum_maximum_fusion
  66.2 0.4 fusion.62
  66.6 1.0 %fusion.30 = f32[9,9,128,24]{2,3,1,0:T(8,128)S(1)} fusion(f32[24,3,1,1]{0,1,3,2:T(4,128)S(1)} %copy-done.10, f32[5,10,9,128]{3,0,2,1:T(8,128)S(1)} %get-tuple-element.113), kind=kOutput, calls=%fused_computation.47 | convolution fusion | flops 8957952 | bytes 1163264 | tf_op jit(solution)/shard_map/ij,jxyz->ixyz/dot_general | solution.py:88
  67.6 1.0 %fusion.33 = f32[24,9,9,128]{3,0,2,1:T(8,128)S(1)} fusion(f32[24,3,1,1]{0,1,3,2:T(4,128)S(1)} %copy-done.9, f32[3,9,9,127]{3,0,2,1:T(4,128)S(1)} %get-tuple-element.137), kind=kOutput, calls=%fused_computation.50 | convolution fusion | flops 8957952 | bytes 1119060 | tf_op jit(solution)/shard_map/ij,jxyz->ixyz/dot_general | solution.py:88
  68.7 1.0 %fusion.36 = f32[9,9,128,24]{2,3,1,0:T(8,128)S(1)} fusion(f32[24,3,1,1]{0,1,3,2:T(4,128)S(1)} %copy-done.8, f32[3,9,9,127]{3,0,2,1:T(4,128)S(1)} %get-tuple-element.138), kind=kOutput, calls=%fused_computation.53 | convolution fusion | flops 8957952 | bytes 1119060 | tf_op jit(solution)/shard_map/ij,jxyz->ixyz/dot_general | solution.py:88
  69.7 1.0 %fusion.38 = f32[9,9,128,24]{2,3,1,0:T(8,128)S(1)} fusion(f32[24,3,1,1]{0,1,3,2:T(4,128)S(1)} %copy-done.7, f32[3,9,9,127]{3,0,2,1:T(4,128)S(1)} %get-tuple-element.107), kind=kOutput, calls=%fused_computation.55 | convolution fusion | flops 8957952 | bytes 1119060 | tf_op jit(solution)/shard_map/ij,jxyz->ixyz/dot_general | solution.py:88
  70.7 1.1 %fusion.16 = f32[9,9,128,24]{2,3,1,0:T(8,128)S(1)} fusion(f32[9,9,128,24]{2,3,1,0:T(8,128)S(1)} %fusion.36, f32[9,9,128,24]{2,3,1,0:T(8,128)S(1)} %fusion.30, f32[9,9,128,24]{2,3,1,0:T(8,128)S(1)} %fusion.38, f32[24,3,1,1]{0,1,3,2:T(4,128)S(1)} %copy-done.6, f32[5,10,9,128]{3,0,2,1:T(8,128)S(1)} %get-tuple-element.112), kind=kOutput, calls=%fused_computation.30 | convolution fusion | flops 9704448 | bytes 4149248 | tf_op jit(solution)/shard_map/ij,jxyz->ixyz/dot_general | solution.py:88
  71.9 1.0 %fusion.14 = f32[24,9,9,128]{3,0,2,1:T(8,128)S(1)} fusion(f32[9,9,128,24]{2,3,1,0:T(8,128)S(1)} %fusion.16, f32[24,3,1,1]{0,1,3,2:T(4,128)S(1)} %copy-done.13, f32[5,10,9,128]{3,0,2,1:T(8,128)S(1)} %get-tuple-element.112), kind=kOutput, calls=%fused_computation.27 | convolution fusion | flops 9206784 | bytes 2158592 | tf_op jit(solution)/shard_map/ij,jxyz->ixyz/dot_general | solution.py:88
  72.9 1.0 %convolution_add_fusion.1 = f32[24,9,9,128]{3,0,2,1:T(8,128)S(1)} fusion(f32[24,9,9,128]{3,0,2,1:T(8,128)S(1)} %fusion.14, f32[24,3,1,1]{0,1,3,2:T(4,128)S(1)} %copy-done.12, f32[3,9,9,127]{3,0,2,1:T(4,128)S(1)} %get-tuple-element.106), kind=kOutput, calls=%fused_computation.25 | convolution fusion | flops 9206784 | bytes 2114388 | tf_op jit(solution)/shard_map/ij,jxyz->ixyz/dot_general | solution.py:88
  74.0 1.1 %fusion.13 = f32[24,9,9,128]{3,0,2,1:T(8,128)S(1)} fusion(f32[24,9,9,128]{3,0,2,1:T(8,128)S(1)} %fusion.33, f32[24,9,9,128]{3,0,2,1:T(8,128)S(1)} %convolution_add_fusion.1, f32[24,3,1,1]{0,1,3,2:T(4,128)S(1)} %copy-done.11, f32[9,9,128]{2,1,0:T(8,128)S(1)} %slice.251, f32[5,10,9,128]{3,0,2,1:T(8,128)S(1)} %get-tuple-element.113), kind=kOutput, calls=%fused_computation.24 | convolution fusion | flops 9704448 | bytes 3227648 | tf_op jit(solution)/shard_map/ij,jxyz->ixyz/dot_general | solution.py:88
  75.1 0.1 fusion.61
  75.3 0.1 fusion.46
  75.4 3.1 %fusion.6 = f32[3,8,8,128]{3,2,1,0:T(8,128)S(1)} fusion(f32[8,8,4096]{2,1,0:T(8,128)S(1)} %get-tuple-element.115, f32[3,4096]{1,0:T(4,128)S(1)} %bitcast.133, f32[4096]{0:T(1024)S(1)} %bitcast.141, s32[4096]{0:T(1024)S(1)} %bitcast.147, f32[4096]{0:T(1024)S(1)} %broadcast_subtract_fusion.2, s32[4096]{0:T(1024)S(1)} %bitcast.149), kind=kOutput, calls=%fused_computation.12 | convolution fusion | flops 1211367424 | bytes 1261568 | tf_op jit(solution)/shard_map/dot_general | solution.py:144
  78.6 0.5 multiply_add_fusion
  79.1 0.6 copy.45
  79.7 0.6 copy.46
  (85 shorter events, 1.3 us)
Async XLA Ops:
  0.6 10.4 %copy-start.1 = (f32[3,8,8,128]{3,2,1,0:T(8,128)S(1)}, f32[3,8,8,128]{3,2,1,0:T(8,128)}, u32[]{:S(2)}) copy-start(f32[3,8,8,128]{3,2,1,0:T(8,128)} %param.15) | copy-start | bytes 294916
  4.0 18.8 %collective-permute-start.1 = (f32[5,1,8,128]{3,0,2,1:T(8,128)S(1)}, f32[5,1,8,128]{3,0,2,1:T(8,128)S(1)}, u32[]{:S(2)}, u32[]{:S(2)}) collective-permute-start(f32[5,1,8,128]{3,0,2,1:T(8,128)S(1)} %get-tuple-element.119), channel_id=1, source_target_pairs={{4,0},{8,4},{12,8},{16,12},{20,16},{24,20},{28,24},{5,1},{9,5},{13... | collective-permute-start | bytes 61448 | tf_op jit(solution)/shard_map/ppermute | solution.py:22
  5.3 17.5 %collective-permute-start = (f32[5,1,8,128]{3,0,2,1:T(8,128)S(1)}, f32[5,1,8,128]{3,0,2,1:T(8,128)S(1)}, u32[]{:S(2)}, u32[]{:S(2)}) collective-permute-start(f32[5,1,8,128]{3,0,2,1:T(8,128)S(1)} %get-tuple-element.118), channel_id=1, source_target_pairs={{0,4},{4,8},{8,12},{12,16},{16,20},{20,24},{24,28},{1,5},{5,9},{9,... | collective-permute-start | bytes 61448 | tf_op jit(solution)/shard_map/ppermute | solution.py:19
  14.3 6.9 %copy-start.4 = (f32[2,16,1,128]{3,2,1,0:T(1,128)S(1)}, f32[2,16,1,128]{3,2,1,0:T(1,128)}, u32[]{:S(2)}) copy-start(f32[2,16,1,128]{3,2,1,0:T(1,128)} %param.23) | copy-start | bytes 49156
  14.3 7.8 %copy-start.5 = (s32[16,1,128]{2,1,0:T(1,128)S(1)}, s32[16,1,128]{2,1,0:T(1,128)}, u32[]{:S(2)}) copy-start(s32[16,1,128]{2,1,0:T(1,128)} %param.22) | copy-start | bytes 24580
  14.3 8.5 %copy-start = (f32[8,8,128]{2,1,0:T(8,128)S(1)}, f32[8,8,128]{2,1,0:T(8,128)}, u32[]{:S(2)}) copy-start(f32[8,8,128]{2,1,0:T(8,128)} %param.18) | copy-start | bytes 98308
  15.4 13.3 %all-to-all-start = ((f32[3,8,512]{2,0,1:T(4,128)}), f32[3,8,512]{2,0,1:T(4,128)S(1)}, u32[]{:S(2)}, u32[]{:S(2)}) async-start(f32[3,8,512]{2,0,1:T(4,128)} %bitcast.39), calls=%async_computation | async-start | bytes 131072 | tf_op jit(solution)/shard_map/all_to_all | solution.py:218
  22.8 43.0 %collective-permute-start.3 = (f32[5,10,1,128]{3,0,2,1:T(8,128)S(1)}, f32[5,10,1,128]{3,0,2,1:T(8,128)S(1)}, u32[]{:S(2)}, u32[]{:S(2)}) collective-permute-start(f32[5,10,1,128]{3,0,2,1:T(8,128)S(1)} %get-tuple-element.117), channel_id=1, source_target_pairs={{1,0},{2,1},{3,2},{5,4},{6,5},{7,6},{9,8},{10,9},{11,10},{13,12},{... | collective-permute-start | bytes 76808 | tf_op jit(solution)/shard_map/ppermute | solution.py:22
  24.1 41.7 %collective-permute-start.2 = (f32[5,10,1,128]{3,0,2,1:T(8,128)S(1)}, f32[5,10,1,128]{3,0,2,1:T(8,128)S(1)}, u32[]{:S(2)}, u32[]{:S(2)}) collective-permute-start(f32[5,10,1,128]{3,0,2,1:T(8,128)S(1)} %get-tuple-element.116), channel_id=1, source_target_pairs={{0,1},{1,2},{2,3},{4,5},{5,6},{6,7},{8,9},{9,10},{10,11},{12,13},{... | collective-permute-start | bytes 76808 | tf_op jit(solution)/shard_map/ppermute | solution.py:19
  28.7 16.3 %copy-start.14 = (f32[16,1]{0,1:T(1,128)S(1)}, f32[16,1]{0,1:T(1,128)}, u32[]{:S(2)}) copy-start(f32[16,1]{0,1:T(1,128)} %param.24) | copy-start | bytes 196
  61.5 5.1 %copy-start.10 = (f32[24,3,1,1]{0,1,3,2:T(4,128)S(1)}, f32[24,3,1,1]{0,1,3,2:T(4,128)}, u32[]{:S(2)}) copy-start(f32[24,3,1,1]{0,1,3,2:T(4,128)} %constant.139) | copy-start | bytes 868
  61.5 13.9 %all-to-all-start.1 = ((f32[3,8,512]{2,0,1:T(4,128)}), f32[3,8,512]{2,0,1:T(4,128)S(1)}, u32[]{:S(2)}, u32[]{:S(2)}) async-start(f32[3,8,512]{2,0,1:T(4,128)} %bitcast.46), calls=%async_computation.1 | async-start | bytes 131072 | tf_op jit(solution)/shard_map/all_to_all | solution.py:224
  66.0 1.6 %copy-start.9 = (f32[24,3,1,1]{0,1,3,2:T(4,128)S(1)}, f32[24,3,1,1]{0,1,3,2:T(4,128)}, u32[]{:S(2)}) copy-start(f32[24,3,1,1]{0,1,3,2:T(4,128)} %constant.144) | copy-start | bytes 868
  66.1 2.5 %copy-start.8 = (f32[24,3,1,1]{0,1,3,2:T(4,128)S(1)}, f32[24,3,1,1]{0,1,3,2:T(4,128)}, u32[]{:S(2)}) copy-start(f32[24,3,1,1]{0,1,3,2:T(4,128)} %constant.140) | copy-start | bytes 868
  66.6 3.1 %copy-start.7 = (f32[24,3,1,1]{0,1,3,2:T(4,128)S(1)}, f32[24,3,1,1]{0,1,3,2:T(4,128)}, u32[]{:S(2)}) copy-start(f32[24,3,1,1]{0,1,3,2:T(4,128)} %constant.138) | copy-start | bytes 868
  67.6 3.1 %copy-start.6 = (f32[24,3,1,1]{0,1,3,2:T(4,128)S(1)}, f32[24,3,1,1]{0,1,3,2:T(4,128)}, u32[]{:S(2)}) copy-start(f32[24,3,1,1]{0,1,3,2:T(4,128)} %constant.137) | copy-start | bytes 868
  70.7 1.2 %copy-start.13 = (f32[24,3,1,1]{0,1,3,2:T(4,128)S(1)}, f32[24,3,1,1]{0,1,3,2:T(4,128)}, u32[]{:S(2)}) copy-start(f32[24,3,1,1]{0,1,3,2:T(4,128)} %constant.141) | copy-start | bytes 868
  71.9 1.1 %copy-start.12 = (f32[24,3,1,1]{0,1,3,2:T(4,128)S(1)}, f32[24,3,1,1]{0,1,3,2:T(4,128)}, u32[]{:S(2)}) copy-start(f32[24,3,1,1]{0,1,3,2:T(4,128)} %constant.142) | copy-start | bytes 868
  71.9 2.1 %copy-start.11 = (f32[24,3,1,1]{0,1,3,2:T(4,128)S(1)}, f32[24,3,1,1]{0,1,3,2:T(4,128)}, u32[]{:S(2)}) copy-start(f32[24,3,1,1]{0,1,3,2:T(4,128)} %constant.143) | copy-start | bytes 868
  75.4 3.1 %copy-start.2 = (f32[3,8,8,128]{3,2,1,0:T(8,128)S(1)}, f32[3,8,8,128]{3,2,1,0:T(8,128)}, u32[]{:S(2)}) copy-start(f32[3,8,8,128]{3,2,1,0:T(8,128)} %param.17) | copy-start | bytes 294916
  75.4 3.1 %copy-start.3 = (f32[3,8,8,128]{3,2,1,0:T(8,128)S(1)}, f32[3,8,8,128]{3,2,1,0:T(8,128)}, u32[]{:S(2)}) copy-start(f32[3,8,8,128]{3,2,1,0:T(8,128)} %param.16) | copy-start | bytes 294916
where the time goes:
time: 81.2 us; the launch traced here: 80.4 us
  matrix products  46.3 us (57%)
  starting transfers between devices  20.3 us (25%)
  other arithmetic  7.03 us (9%)
  local copies, waits for them, and re-layouts  5.35 us (7%)
  between operations  1.21 us (1%)
    dot_general x4, matrix products, place_single(): jnp.dot(stretch_values, onehot, precision=lax.Precision.HIGHEST)  16.2 us
    dot_general x4, matrix products, pick_single(): return jnp.dot(places, onehot.T, precision=lax.Precision.HIGHEST)  15.4 us
    dot_general x8, matrix products, element_forces(): jnp.einsum('ij,jxyz->ixyz', table[:, 3 * corner:3 * corner + 3], local, p...  8.33 us
    ppermute x2, starting transfers between devices, padded_2(): lax.ppermute(lax.slice_in_dim(block, block.shape[dim] - width, None, axis...  7.58 us
    all_to_all x1, starting transfers between devices, shards(): lax.all_to_all(places.reshape(3, parts, -1), 'dom', split_axis=1, concat_...  5.79 us
    all_to_all x1, starting transfers between devices, shards(): lax.all_to_all(pulls.reshape(3, parts, -1), 'dom', split_axis=1, concat_a...  4.32 us
    dot_general x1, matrix products, interpolate(): jnp.dot(field.reshape(3 * width * height, depth), weight_z, precision=lax...  3.27 us
    dot_general x1, matrix products, spread(): summed = jnp.dot(terms, weight_z.T, precision=lax.Precision.HIGHEST)  3.11 us
  transfers between devices with their start and end apart: 6, of which 0 were waited for; matrix products, arithmetic and copies ran while one was open for 63% of the time, Pallas kernels for 0%

commit v1 on v0

--- a/solution.py
+++ b/solution.py
@@ -145,33 +145,30 @@
     return summed.reshape(3, width, height, depth)
 
 
+def split_onehots(wanted, total):
+    lanes = math.gcd(total, 128)
+    low = (
+        lax.broadcasted_iota(jnp.int32, (lanes, wanted.shape[0]), 0) == (wanted % lanes)[None]
+    ).astype(jnp.float32)
+    high = lax.broadcasted_iota(jnp.int32, (total // lanes, wanted.shape[0]), 0) == (
+        wanted // lanes
+    )[None]
+    return low, high
+
+
 def pick_rows(places, wanted, span_rows):
     total = places.shape[1]
-    groups = wanted.reshape(-1, span_rows)
-
-    def pick_single(members):
-        onehot = (
-            members[:, None] == lax.broadcasted_iota(jnp.int32, (span_rows, total), 1)
-        ).astype(jnp.float32)
-        return jnp.dot(places, onehot.T, precision=lax.Precision.HIGHEST)
-
-    picked = lax.map(pick_single, groups)
-    return picked.transpose(1, 0, 2).reshape(3, -1)
+    low, high = split_onehots(wanted, total)
+    rows, lanes = high.shape[0], low.shape[0]
+    spread_rows = jnp.dot(places.reshape(3 * rows, lanes), low, precision=lax.Precision.HIGHEST)
+    return jnp.sum(jnp.where(high[None], spread_rows.reshape(3, rows, -1), 0.0), axis=1)
 
 
 def place_rows(values, wanted, total, span_rows):
-    groups = wanted.reshape(-1, span_rows)
-    pieces = values.reshape(3, -1, span_rows).transpose(1, 0, 2)
-
-    def place_single(carry, item):
-        members, stretch_values = item
-        onehot = (
-            members[:, None] == lax.broadcasted_iota(jnp.int32, (span_rows, total), 1)
-        ).astype(jnp.float32)
-        return (carry + jnp.dot(stretch_values, onehot, precision=lax.Precision.HIGHEST), None)
-
-    result, _ = lax.scan(place_single, jnp.zeros((3, total), jnp.float32), (groups, pieces))
-    return result
+    low, high = split_onehots(wanted, total)
+    rows, lanes = high.shape[0], low.shape[0]
+    terms = jnp.where(high[None], values[:, None, :], 0.0).reshape(3 * rows, -1)
+    return jnp.dot(terms, low.T, precision=lax.Precision.HIGHEST).reshape(3, total)
 
 
 def fibre_forces(places, slots, angles, stiffness):

time: 81.2 us -> 49.8 us (0.61)
  matrix products: 46.3 us -> 16.1 us
    dot_general x8 -> x2, matrix products: 31.6 us -> 1.34 us  [the longest x1 0.74 us: place_rows(): jnp.dot(terms, low.T, precision=lax.Precision.HIGHEST).reshape(3, total)]
    unnamed x36 -> x37, local copies, waits for them, and re-layouts: 2.92 us -> 2.4 us
  transfers between devices with their start and end apart: 6 -> 6, of which waited for: 0 -> 0; matrix products, arithmetic and copies ran while one was open for 63% -> 39% of each run, Pallas kernels for 0% -> 0%
where the time goes in v1:
time: 49.8 us; the launch traced here: 48.9 us
  starting transfers between devices  20.2 us (41%)
  matrix products  16.1 us (32%)
  other arithmetic  6.49 us (13%)
  local copies, waits for them, and re-layouts  4.96 us (10%)
  between operations  1.21 us (2%)
    dot_general x8, matrix products, element_forces(): jnp.einsum('ij,jxyz->ixyz', table[:, 3 * corner:3 * corner + 3], local, p...  8.33 us
    ppermute x2, starting transfers between devices, padded_2(): lax.ppermute(lax.slice_in_dim(block, block.shape[dim] - width, None, axis...  7.58 us
    all_to_all x1, starting transfers between devices, shards(): lax.all_to_all(places.reshape(3, parts, -1), 'dom', split_axis=1, concat_...  5.79 us
    all_to_all x1, starting transfers between devices, shards(): lax.all_to_all(pulls.reshape(3, parts, -1), 'dom', split_axis=1, concat_a...  4.19 us
    dot_general x1, matrix products, interpolate(): jnp.dot(field.reshape(3 * width * height, depth), weight_z, precision=lax...  3.27 us
    dot_general x1, matrix products, spread(): summed = jnp.dot(terms, weight_z.T, precision=lax.Precision.HIGHEST)  3.11 us
    ppermute x2, starting transfers between devices, padded_2(): lax.ppermute(lax.slice_in_dim(block, 0, width, axis=dim), axis, backward)  2.58 us
    unnamed x37, local copies, waits for them, and re-layouts  2.4 us
  transfers between devices with their start and end apart: 6, of which 0 were waited for; matrix products, arithmetic and copies ran while one was open for 39% of the time, Pallas kernels for 0%

profile of v1, /device:TPU:0, one launch (start us, length us, event | category | flops | bytes accessed | tf_op | source)
XLA Modules:
  0.0 48.9 jit_solution(1424179783037810465)
XLA Ops:
  0.6 0.7 %fusion.57 = f32[16]{0:T(128)S(1)} fusion(s32[1,1,16]{2,1,0:T(1,128)} %param.15), kind=kLoop, calls=%fused_computation.142 | loop fusion | flops 128 | bytes 128 | tf_op jit(solution)/shard_map/broadcast_in_dim | solution.py:69
  1.3 0.1 broadcast_in_dim.137
  1.4 0.1 broadcast_in_dim.138
  1.5 1.0 %copy.42 = f32[3,8,8,128]{3,0,2,1:T(4,128)S(1)} copy(f32[3,8,8,128]{3,2,1,0:T(8,128)} %param.11) | data formatting | bytes 196608 | tf_op args[0]
  2.5 0.8 %multiply_multiply_fusion = f32[8,8,128]{2,1,0:T(8,128)S(1)} fusion(f32[8,8,128]{2,1,0:T(8,128)} %param.14, f32[128]{0:T(128)S(1)} %broadcast_in_dim.138), kind=kLoop, calls=%fused_computation.88 | loop fusion | flops 16384 | bytes 66048 | tf_op jit(solution)/shard_map/mul | solution.py:210
  3.2 0.7 %pad_maximum_fusion.15 = (f32[5,1,8,128]{3,0,2,1:T(8,128)S(1)}, f32[5,1,8,128]{3,0,2,1:T(8,128)S(1)}) fusion(f32[1,8,8,128]{3,0,2,1:T(1,128)} %bitcast.98, f32[1,8,8,128]{3,0,2,1:T(1,128)S(1)} %bitcast.102, f32[3,8,8,128]{3,0,2,1:T(4,128)S(1)} %copy.42), kind=kLoop, calls=%fused_computation.105 | loop fusion | flops 20480 | bytes 204800 | tf_op jit(solution)/shard_map/slice | solution.py:20
  4.0 1.3 %collective-permute-start.1 = (f32[5,1,8,128]{3,0,2,1:T(8,128)S(1)}, f32[5,1,8,128]{3,0,2,1:T(8,128)S(1)}, u32[]{:S(2)}, u32[]{:S(2)}) collective-permute-start(f32[5,1,8,128]{3,0,2,1:T(8,128)S(1)} %get-tuple-element.34), channel_id=1, source_target_pairs={{4,0},{8,4},{12,8},{16,12},{20,16},{24,20},{28,24},{5,1},{9,5},{13... | collective-permute-start | bytes 61448 | tf_op jit(solution)/shard_map/ppermute | solution.py:22
  5.3 3.0 %collective-permute-start = (f32[5,1,8,128]{3,0,2,1:T(8,128)S(1)}, f32[5,1,8,128]{3,0,2,1:T(8,128)S(1)}, u32[]{:S(2)}, u32[]{:S(2)}) collective-permute-start(f32[5,1,8,128]{3,0,2,1:T(8,128)S(1)} %get-tuple-element.33), channel_id=1, source_target_pairs={{0,4},{4,8},{8,12},{12,16},{16,20},{20,24},{24,28},{1,5},{5,9},{9,... | collective-permute-start | bytes 61448 | tf_op jit(solution)/shard_map/ppermute | solution.py:19
  8.3 0.8 %fusion.68 = (f32[1,1,4096]{2,1,0:T(1,128)S(1)}, f32[1,1,4096]{2,1,0:T(1,128)S(1)}, f32[1,1,4096]{2,1,0:T(1,128)S(1)}) fusion(f32[3,1,4096]{2,1,0:T(1,128)} %param.17), kind=kLoop, calls=%fused_computation.155 | loop fusion | bytes 98304 | tf_op jit(solution)/shard_map/slice | solution.py:129
  9.1 0.8 %broadcast_add_fusion.1 = (s32[1,4096]{1,0:T(1,128)S(1)}, s32[1,4096]{1,0:T(1,128)S(1)}, s32[1,4096]{1,0:T(1,128)S(1)}, s32[1,4096]{1,0:T(1,128)S(1)}, s32[1,4096]{1,0:T(1,128)S(1)}) fusion(s32[1,4096]{1,0:T(1,128)} %param.16), kind=kLoop, calls=%fused_computation.126 | loop fusion | flops 102400 | bytes 98304 | tf_op jit(solution)/shard_map/add | solution.py:118
  9.9 0.8 %broadcast_add_fusion = (s32[1,4096]{1,0:T(1,128)S(1)}, s32[1,4096]{1,0:T(1,128)S(1)}) fusion(s32[1,4096]{1,0:T(1,128)} %param.16, s32[1,4096]{1,0:T(1,128)S(1)} %get-tuple-element.48), kind=kLoop, calls=%fused_computation.125 | loop fusion | flops 98304 | bytes 65536 | tf_op jit(solution)/shard_map/add | solution.py:118
  10.8 0.1 select_add_fusion.3
  10.9 0.1 fusion.27
  11.0 3.3 %fusion.3 = f32[4096,192]{0,1:T(8,128)S(1)} fusion(f32[192,128]{1,0:T(8,128)S(1)} %bitcast.106, f32[4096]{0:T(1024)S(1)} %bitcast.127, s32[4096]{0:T(1024)S(1)} %bitcast.131, f32[4096]{0:T(1024)S(1)} %broadcast_subtract_fusion.2, s32[4096]{0:T(1024)S(1)} %bitcast.133), kind=kOutput, calls=%fused_computation.7 | convolution fusion | flops 1210580992 | bytes 3309568 | tf_op jit(solution)/shard_map/dot_general | solution.py:136
  14.3 1.0 %multiply_reduce_fusion = f32[3,4096]{1,0:T(4,128)} fusion(f32[3,64,4096]{2,1,0:T(8,128)S(1)} %bitcast.95, f32[64,4096]{1,0:T(8,128)S(1)} %get-tuple-element.29), kind=kLoop, calls=%fused_computation.2 | loop fusion | flops 1560576 | bytes 4243456 | tf_op jit(solution)/shard_map/reduce_sum | solution.py:139
  15.4 5.8 %all-to-all-start = ((f32[3,8,512]{2,0,1:T(4,128)}), f32[3,8,512]{2,0,1:T(4,128)S(1)}, u32[]{:S(2)}, u32[]{:S(2)}) async-start(f32[3,8,512]{2,0,1:T(4,128)} %bitcast.40), calls=%async_computation | async-start | bytes 131072 | tf_op jit(solution)/shard_map/all_to_all | solution.py:215
  21.2 0.2 fusion.69
  21.5 0.1 multiply_bitcast_fusion.1
  21.6 1.3 %collective-permute-start.3 = (f32[5,10,1,128]{3,0,2,1:T(8,128)S(1)}, f32[5,10,1,128]{3,0,2,1:T(8,128)S(1)}, u32[]{:S(2)}, u32[]{:S(2)}) collective-permute-start(f32[5,10,1,128]{3,0,2,1:T(8,128)S(1)} %get-tuple-element.32), channel_id=1, source_target_pairs={{1,0},{2,1},{3,2},{5,4},{6,5},{7,6},{9,8},{10,9},{11,10},{13,12},{... | collective-permute-start | bytes 76808 | tf_op jit(solution)/shard_map/ppermute | solution.py:22
  22.9 4.5 %collective-permute-start.2 = (f32[5,10,1,128]{3,0,2,1:T(8,128)S(1)}, f32[5,10,1,128]{3,0,2,1:T(8,128)S(1)}, u32[]{:S(2)}, u32[]{:S(2)}) collective-permute-start(f32[5,10,1,128]{3,0,2,1:T(8,128)S(1)} %get-tuple-element.31), channel_id=1, source_target_pairs={{0,1},{1,2},{2,3},{4,5},{5,6},{6,7},{8,9},{9,10},{10,11},{12,13},{... | collective-permute-start | bytes 76808 | tf_op jit(solution)/shard_map/ppermute | solution.py:19
  27.5 0.6 %fusion.11 = f32[3,2048]{1,0:T(4,128)S(1)} fusion(f32[3,32,128]{2,1,0:T(8,128)S(1)} %dot_general.59, s32[2048]{0:T(1024)S(1)} %get-tuple-element.50, pred[32,2048]{1,0:T(8,128)(4,1)S(1)} %iota_compare_fusion.8), kind=kOutput, calls=%fused_computation.20 | convolution fusion | flops 302639104 | bytes 147456 | tf_op jit(solution)/shard_map/dot_general | solution.py:163
  28.2 0.1 slice.262
  28.2 0.1 slice.261
  28.3 0.1 fusion.50
  28.4 0.1 multiply_select_fusion
  28.5 0.1 subtract_bitcast_fusion
  28.6 0.1 broadcast_select_fusion
  28.7 0.0 copy-start.7
  28.7 0.7 %fusion.12 = f32[96,128]{1,0:T(8,128)S(1)} fusion(f32[96,2048]{1,0:T(8,128)S(1)} %bitcast.94, s32[2048]{0:T(1024)S(1)} %get-tuple-element.50), kind=kOutput, calls=%fused_computation.22 | convolution fusion | flops 302252032 | bytes 843776 | tf_op jit(solution)/shard_map/dot_general | solution.py:171
  29.4 0.7 %copy.38 = f32[3,8,512]{2,0,1:T(4,128)} copy(f32[3,8,512]{2,1,0:T(8,128)S(1)} %reshape_reshape.4) | data formatting | bytes 98304 | tf_op jit(solution)/shard_map/reshape;reshape | solution.py:222
  30.1 4.2 %all-to-all-start.1 = ((f32[3,8,512]{2,0,1:T(4,128)}), f32[3,8,512]{2,0,1:T(4,128)S(1)}, u32[]{:S(2)}, u32[]{:S(2)}) async-start(f32[3,8,512]{2,0,1:T(4,128)} %copy.38), calls=%async_computation.1 | async-start | bytes 131072 | tf_op jit(solution)/shard_map/all_to_all | solution.py:221
  34.3 0.2 pad_maximum_fusion.7
  34.5 0.1 maximum_maximum_fusion
  34.7 0.4 fusion.65
  35.1 1.0 %fusion.30 = f32[9,9,128,24]{2,3,1,0:T(8,128)S(1)} fusion(f32[24,3,1,1]{0,1,3,2:T(4,128)S(1)} %copy-done.7, f32[5,10,9,128]{3,0,2,1:T(8,128)S(1)} %get-tuple-element.28), kind=kOutput, calls=%fused_computation.44 | convolution fusion | flops 8957952 | bytes 1163264 | tf_op jit(solution)/shard_map/ij,jxyz->ixyz/dot_general | solution.py:88
  36.2 1.0 %fusion.33 = f32[24,9,9,128]{3,0,2,1:T(8,128)S(1)} fusion(f32[24,3,1,1]{0,1,3,2:T(4,128)S(1)} %copy-done.10, f32[3,9,9,127]{3,0,2,1:T(4,128)S(1)} %get-tuple-element.53), kind=kOutput, calls=%fused_computation.47 | convolution fusion | flops 8957952 | bytes 1119060 | tf_op jit(solution)/shard_map/ij,jxyz->ixyz/dot_general | solution.py:88
  37.2 1.0 %fusion.36 = f32[9,9,128,24]{2,3,1,0:T(8,128)S(1)} fusion(f32[24,3,1,1]{0,1,3,2:T(4,128)S(1)} %copy-done.9, f32[3,9,9,127]{3,0,2,1:T(4,128)S(1)} %get-tuple-element.54), kind=kOutput, calls=%fused_computation.50 | convolution fusion | flops 8957952 | bytes 1119060 | tf_op jit(solution)/shard_map/ij,jxyz->ixyz/dot_general | solution.py:88
  38.2 1.0 %fusion.38 = f32[9,9,128,24]{2,3,1,0:T(8,128)S(1)} fusion(f32[24,3,1,1]{0,1,3,2:T(4,128)S(1)} %copy-done.8, f32[3,9,9,127]{3,0,2,1:T(4,128)S(1)} %get-tuple-element.22), kind=kOutput, calls=%fused_computation.52 | convolution fusion | flops 8957952 | bytes 1119060 | tf_op jit(solution)/shard_map/ij,jxyz->ixyz/dot_general | solution.py:88
  39.2 1.1 %fusion.10 = f32[9,9,128,24]{2,3,1,0:T(8,128)S(1)} fusion(f32[9,9,128,24]{2,3,1,0:T(8,128)S(1)} %fusion.36, f32[9,9,128,24]{2,3,1,0:T(8,128)S(1)} %fusion.30, f32[9,9,128,24]{2,3,1,0:T(8,128)S(1)} %fusion.38, f32[24,3,1,1]{0,1,3,2:T(4,128)S(1)} %copy-done.6, f32[5,10,9,128]{3,0,2,1:T(8,128)S(1)} %get-tuple-element.27), kind=kOutput, calls=%fused_computation.19 | convolution fusion | flops 9704448 | bytes 4149248 | tf_op jit(solution)/shard_map/ij,jxyz->ixyz/dot_general | solution.py:88
  40.4 1.0 %fusion.8 = f32[24,9,9,128]{3,0,2,1:T(8,128)S(1)} fusion(f32[9,9,128,24]{2,3,1,0:T(8,128)S(1)} %fusion.10, f32[24,3,1,1]{0,1,3,2:T(4,128)S(1)} %copy-done.13, f32[5,10,9,128]{3,0,2,1:T(8,128)S(1)} %get-tuple-element.27), kind=kOutput, calls=%fused_computation.16 | convolution fusion | flops 9206784 | bytes 2158592 | tf_op jit(solution)/shard_map/ij,jxyz->ixyz/dot_general | solution.py:88
  41.5 1.0 %convolution_add_fusion.1 = f32[24,9,9,128]{3,0,2,1:T(8,128)S(1)} fusion(f32[24,9,9,128]{3,0,2,1:T(8,128)S(1)} %fusion.8, f32[24,3,1,1]{0,1,3,2:T(4,128)S(1)} %copy-done.12, f32[3,9,9,127]{3,0,2,1:T(4,128)S(1)} %get-tuple-element.21), kind=kOutput, calls=%fused_computation.14 | convolution fusion | flops 9206784 | bytes 2114388 | tf_op jit(solution)/shard_map/ij,jxyz->ixyz/dot_general | solution.py:88
  42.5 1.1 %fusion.7 = f32[24,9,9,128]{3,0,2,1:T(8,128)S(1)} fusion(f32[24,9,9,128]{3,0,2,1:T(8,128)S(1)} %fusion.33, f32[24,9,9,128]{3,0,2,1:T(8,128)S(1)} %convolution_add_fusion.1, f32[24,3,1,1]{0,1,3,2:T(4,128)S(1)} %copy-done.11, f32[9,9,128]{2,1,0:T(8,128)S(1)} %slice.251, f32[5,10,9,128]{3,0,2,1:T(8,128)S(1)} %get-tuple-element.28), kind=kOutput, calls=%fused_computation.13 | convolution fusion | flops 9704448 | bytes 3227648 | tf_op jit(solution)/shard_map/ij,jxyz->ixyz/dot_general | solution.py:88
  43.6 0.1 fusion.64
  43.8 0.1 fusion.46
  43.9 3.1 %fusion = f32[3,8,8,128]{3,2,1,0:T(8,128)S(1)} fusion(f32[8,8,4096]{2,1,0:T(8,128)S(1)} %get-tuple-element.30, f32[3,4096]{1,0:T(4,128)S(1)} %bitcast.121, f32[4096]{0:T(1024)S(1)} %bitcast.128, s32[4096]{0:T(1024)S(1)} %bitcast.132, f32[4096]{0:T(1024)S(1)} %broadcast_subtract_fusion.2, s32[4096]{0:T(1024)S(1)} %bitcast.134), kind=kOutput, calls=%fused_computation | convolution fusion | flops 1211367424 | bytes 1261568 | tf_op jit(solution)/shard_map/dot_general | solution.py:144
  47.1 0.5 %multiply_add_fusion = (f32[3,8,8,128]{3,0,2,1:T(4,128)S(1)}, f32[3,8,8,128]{3,0,2,1:T(4,128)S(1)}) fusion(f32[3,8,8,128]{3,2,1,0:T(8,128)S(1)} %copy-done.1, f32[8,8,128]{2,1,0:T(8,128)S(1)} %fusion.46, f32[3,8,8,128]{3,2,1,0:T(8,128)S(1)} %fusion, f32[3,8,8,127]{3,0,2,1:T(4,128)S(1)} %get-tuple-element.18, f32[24,9,9,128]{3,0,2,1:T(8,128)S(1)} %fusion.7, ...), kind=kLoop, calls=%fused_computation.66 | loop fusion | flops 393216 | bytes 1405952 | tf_op jit(solution)/shard_map/add | solution.py:230
  47.6 0.6 %copy.43 = f32[3,8,8,128]{3,2,1,0:T(8,128)} copy(f32[3,8,8,128]{3,0,2,1:T(4,128)S(1)} %get-tuple-element.8) | data formatting | bytes 196608
  48.2 0.6 %copy.44 = f32[3,8,8,128]{3,2,1,0:T(8,128)} copy(f32[3,8,8,128]{3,0,2,1:T(4,128)S(1)} %get-tuple-element.9) | data formatting | bytes 196608
  (52 shorter events, 0.3 us)
Async XLA Ops:
  0.6 10.4 %copy-start.1 = (f32[3,8,8,128]{3,2,1,0:T(8,128)S(1)}, f32[3,8,8,128]{3,2,1,0:T(8,128)}, u32[]{:S(2)}) copy-start(f32[3,8,8,128]{3,2,1,0:T(8,128)} %param.11) | copy-start | bytes 294916
  4.0 17.6 %collective-permute-start.1 = (f32[5,1,8,128]{3,0,2,1:T(8,128)S(1)}, f32[5,1,8,128]{3,0,2,1:T(8,128)S(1)}, u32[]{:S(2)}, u32[]{:S(2)}) collective-permute-start(f32[5,1,8,128]{3,0,2,1:T(8,128)S(1)} %get-tuple-element.34), channel_id=1, source_target_pairs={{4,0},{8,4},{12,8},{16,12},{20,16},{24,20},{28,24},{5,1},{9,5},{13... | collective-permute-start | bytes 61448 | tf_op jit(solution)/shard_map/ppermute | solution.py:22
  5.3 16.3 %collective-permute-start = (f32[5,1,8,128]{3,0,2,1:T(8,128)S(1)}, f32[5,1,8,128]{3,0,2,1:T(8,128)S(1)}, u32[]{:S(2)}, u32[]{:S(2)}) collective-permute-start(f32[5,1,8,128]{3,0,2,1:T(8,128)S(1)} %get-tuple-element.33), channel_id=1, source_target_pairs={{0,4},{4,8},{8,12},{12,16},{16,20},{20,24},{24,28},{1,5},{5,9},{9,... | collective-permute-start | bytes 61448 | tf_op jit(solution)/shard_map/ppermute | solution.py:19
  14.3 6.9 %copy-start.4 = (f32[2,16,1,128]{3,2,1,0:T(1,128)S(1)}, f32[2,16,1,128]{3,2,1,0:T(1,128)}, u32[]{:S(2)}) copy-start(f32[2,16,1,128]{3,2,1,0:T(1,128)} %param.19) | copy-start | bytes 49156
  14.3 7.1 %copy-start.5 = (s32[16,1,128]{2,1,0:T(1,128)S(1)}, s32[16,1,128]{2,1,0:T(1,128)}, u32[]{:S(2)}) copy-start(s32[16,1,128]{2,1,0:T(1,128)} %param.18) | copy-start | bytes 24580
  14.3 7.3 %copy-start = (f32[8,8,128]{2,1,0:T(8,128)S(1)}, f32[8,8,128]{2,1,0:T(8,128)}, u32[]{:S(2)}) copy-start(f32[8,8,128]{2,1,0:T(8,128)} %param.14) | copy-start | bytes 98308
  14.3 14.1 %copy-start.14 = (f32[16,1]{0,1:T(1,128)S(1)}, f32[16,1]{0,1:T(1,128)}, u32[]{:S(2)}) copy-start(f32[16,1]{0,1:T(1,128)} %param.20) | copy-start | bytes 196
  15.4 12.1 %all-to-all-start = ((f32[3,8,512]{2,0,1:T(4,128)}), f32[3,8,512]{2,0,1:T(4,128)S(1)}, u32[]{:S(2)}, u32[]{:S(2)}) async-start(f32[3,8,512]{2,0,1:T(4,128)} %bitcast.40), calls=%async_computation | async-start | bytes 131072 | tf_op jit(solution)/shard_map/all_to_all | solution.py:215
  21.6 12.7 %collective-permute-start.3 = (f32[5,10,1,128]{3,0,2,1:T(8,128)S(1)}, f32[5,10,1,128]{3,0,2,1:T(8,128)S(1)}, u32[]{:S(2)}, u32[]{:S(2)}) collective-permute-start(f32[5,10,1,128]{3,0,2,1:T(8,128)S(1)} %get-tuple-element.32), channel_id=1, source_target_pairs={{1,0},{2,1},{3,2},{5,4},{6,5},{7,6},{9,8},{10,9},{11,10},{13,12},{... | collective-permute-start | bytes 76808 | tf_op jit(solution)/shard_map/ppermute | solution.py:22
  22.9 11.4 %collective-permute-start.2 = (f32[5,10,1,128]{3,0,2,1:T(8,128)S(1)}, f32[5,10,1,128]{3,0,2,1:T(8,128)S(1)}, u32[]{:S(2)}, u32[]{:S(2)}) collective-permute-start(f32[5,10,1,128]{3,0,2,1:T(8,128)S(1)} %get-tuple-element.31), channel_id=1, source_target_pairs={{0,1},{1,2},{2,3},{4,5},{5,6},{6,7},{8,9},{9,10},{10,11},{12,13},{... | collective-permute-start | bytes 76808 | tf_op jit(solution)/shard_map/ppermute | solution.py:19
  28.7 6.4 %copy-start.7 = (f32[24,3,1,1]{0,1,3,2:T(4,128)S(1)}, f32[24,3,1,1]{0,1,3,2:T(4,128)}, u32[]{:S(2)}) copy-start(f32[24,3,1,1]{0,1,3,2:T(4,128)} %constant.142) | copy-start | bytes 868
  30.1 13.8 %all-to-all-start.1 = ((f32[3,8,512]{2,0,1:T(4,128)}), f32[3,8,512]{2,0,1:T(4,128)S(1)}, u32[]{:S(2)}, u32[]{:S(2)}) async-start(f32[3,8,512]{2,0,1:T(4,128)} %copy.38), calls=%async_computation.1 | async-start | bytes 131072 | tf_op jit(solution)/shard_map/all_to_all | solution.py:221
  34.5 1.6 %copy-start.10 = (f32[24,3,1,1]{0,1,3,2:T(4,128)S(1)}, f32[24,3,1,1]{0,1,3,2:T(4,128)}, u32[]{:S(2)}) copy-start(f32[24,3,1,1]{0,1,3,2:T(4,128)} %constant.147) | copy-start | bytes 868
  34.7 2.5 %copy-start.9 = (f32[24,3,1,1]{0,1,3,2:T(4,128)S(1)}, f32[24,3,1,1]{0,1,3,2:T(4,128)}, u32[]{:S(2)}) copy-start(f32[24,3,1,1]{0,1,3,2:T(4,128)} %constant.143) | copy-start | bytes 868
  35.1 3.1 %copy-start.8 = (f32[24,3,1,1]{0,1,3,2:T(4,128)S(1)}, f32[24,3,1,1]{0,1,3,2:T(4,128)}, u32[]{:S(2)}) copy-start(f32[24,3,1,1]{0,1,3,2:T(4,128)} %constant.141) | copy-start | bytes 868
  36.1 3.1 %copy-start.6 = (f32[24,3,1,1]{0,1,3,2:T(4,128)S(1)}, f32[24,3,1,1]{0,1,3,2:T(4,128)}, u32[]{:S(2)}) copy-start(f32[24,3,1,1]{0,1,3,2:T(4,128)} %constant.140) | copy-start | bytes 868
  39.2 1.2 %copy-start.13 = (f32[24,3,1,1]{0,1,3,2:T(4,128)S(1)}, f32[24,3,1,1]{0,1,3,2:T(4,128)}, u32[]{:S(2)}) copy-start(f32[24,3,1,1]{0,1,3,2:T(4,128)} %constant.144) | copy-start | bytes 868
  40.4 1.1 %copy-start.12 = (f32[24,3,1,1]{0,1,3,2:T(4,128)S(1)}, f32[24,3,1,1]{0,1,3,2:T(4,128)}, u32[]{:S(2)}) copy-start(f32[24,3,1,1]{0,1,3,2:T(4,128)} %constant.145) | copy-start | bytes 868
  40.4 2.1 %copy-start.11 = (f32[24,3,1,1]{0,1,3,2:T(4,128)S(1)}, f32[24,3,1,1]{0,1,3,2:T(4,128)}, u32[]{:S(2)}) copy-start(f32[24,3,1,1]{0,1,3,2:T(4,128)} %constant.146) | copy-start | bytes 868
  43.9 3.1 %copy-start.2 = (f32[3,8,8,128]{3,2,1,0:T(8,128)S(1)}, f32[3,8,8,128]{3,2,1,0:T(8,128)}, u32[]{:S(2)}) copy-start(f32[3,8,8,128]{3,2,1,0:T(8,128)} %param.13) | copy-start | bytes 294916
  43.9 3.1 %copy-start.3 = (f32[3,8,8,128]{3,2,1,0:T(8,128)S(1)}, f32[3,8,8,128]{3,2,1,0:T(8,128)}, u32[]{:S(2)}) copy-start(f32[3,8,8,128]{3,2,1,0:T(8,128)} %param.12) | copy-start | bytes 294916

commit v2 on v1

v2 whole, which is shorter than its diff:
```python
import functools

import jax
import jax.numpy as jnp
import numpy as np
from jax import lax
from jax.experimental import pallas as pl
from jax.experimental.pallas import tpu as pltpu
from jax.sharding import PartitionSpec as P

class_values = (1.0, 0.45, 0.12)
time_step = 0.25
damping = 0.5
block_edge = 8
lanes = 128
MESH = pl.DeviceIdType.MESH


def stiffness_table():
    poisson = 0.3
    lame = poisson / ((1 + poisson) * (1 - 2 * poisson))
    shear = 0.5 / (1 + poisson)
    elastic = np.zeros((6, 6))
    elastic[:3, :3] = lame
    for place in range(3):
        elastic[place, place] += 2 * shear
        elastic[place + 3, place + 3] = shear
    points = [0.5 - 0.5 / np.sqrt(3.0), 0.5 + 0.5 / np.sqrt(3.0)]
    table = np.zeros((24, 24))
    for gauss_r in points:
        for gauss_p in points:
            for gauss_q in points:
                strain = np.zeros((6, 24))
                for corner in range(8):
                    x_bit, y_bit, z_bit = (corner // 4, corner // 2 % 2, corner % 2)
                    along_r = gauss_r if x_bit else 1 - gauss_r
                    along_p = gauss_p if y_bit else 1 - gauss_p
                    along_q = gauss_q if z_bit else 1 - gauss_q
                    d_x = (2 * x_bit - 1) * along_p * along_q
                    d_y = along_r * (2 * y_bit - 1) * along_q
                    d_z = along_r * along_p * (2 * z_bit - 1)
                    column = 3 * corner
                    strain[0, column] = d_x
                    strain[1, column + 1] = d_y
                    strain[2, column + 2] = d_z
                    strain[3, column] = d_y
                    strain[3, column + 1] = d_x
                    strain[4, column + 1] = d_z
                    strain[4, column + 2] = d_y
                    strain[5, column] = d_z
                    strain[5, column + 2] = d_x
                table += 0.125 * strain.T @ elastic @ strain
    return table


def mode_stiffness():
    single = np.linalg.inv(np.array([[1.0, 1.0], [-1.0, 1.0]]))
    back = np.kron(np.kron(np.kron(single, single), single), np.eye(3))
    table = back.T @ stiffness_table() @ back
    return np.where(np.abs(table) < 1e-12, 0.0, table)


def halves(value):
    high = value.astype(jnp.bfloat16)
    low = (value - high.astype(jnp.float32)).astype(jnp.bfloat16)
    return high, low


def quotient(value, divisor):
    if divisor & (divisor - 1) == 0:
        return lax.shift_right_logical(value, jnp.full_like(value, divisor.bit_length() - 1))
    return lax.div(value, jnp.full_like(value, divisor))


def dot(left, right):
    return jnp.dot(left, right, preferred_element_type=jnp.float32)


def dot_t(left, right):
    return lax.dot_general(
        left, right, (((1,), (1,)), ((), ())), preferred_element_type=jnp.float32
    )


def kernel(
    parts,
    columns,
    class_ref,
    displacement_ref,
    velocity_ref,
    load_ref,
    density_ref,
    element_ref,
    coords_ref,
    slot_ref,
    angle_ref,
    stiffness_ref,
    new_displacement_ref,
    new_velocity_ref,
    fields,
    y_send,
    y_recv,
    x_recv,
    weight_z,
    weight_x,
    weight_y,
    onehot,
    angles,
    picked,
    nodes,
    send_out,
    recv_out,
    send_back,
    recv_back,
    total,
    elastic,
    mass,
    y_sems,
    x_sems,
    out_send_sems,
    out_recv_sems,
    back_send_sems,
    back_recv_sems,
):
    _, width, height, depth = displacement_ref.shape
    rows = fields.shape[2]
    cap = recv_out.shape[2]
    slot_rows = cap // lanes
    all_rows = parts * slot_rows
    fibres = slot_ref.shape[0]
    me = lax.axis_index("dom")
    column = lax.axis_index("blk")

    barrier = pltpu.get_barrier_semaphore()

    def greet(step, carry):
        other = lax.rem(me + step, parts)
        pl.semaphore_signal(barrier, inc=1, device_id=(other, column), device_id_type=MESH)
        return carry

    lax.fori_loop(1, parts, greet, 0)

    @pl.when(column > 0)
    def _():
        pl.semaphore_signal(barrier, inc=1, device_id=(me, column - 1), device_id_type=MESH)

    @pl.when(column < columns - 1)
    def _():
        pl.semaphore_signal(barrier, inc=1, device_id=(me, column + 1), device_id_type=MESH)

    block_of = quotient(lax.broadcasted_iota(jnp.int32, (1, depth), 1), block_edge)
    for x in range(width):
        for y_block in range(height // block_edge):
            classes = jnp.zeros((1, depth), jnp.int32)
            for z_block in range(depth // block_edge):
                classes = jnp.where(
                    block_of == z_block, class_ref[x // block_edge, y_block, z_block], classes
                )
            factor = jnp.zeros((1, depth), jnp.float32)
            for index, value in enumerate(class_values):
                factor = jnp.where(classes == index, jnp.float32(value), factor)
            span = slice(y_block * block_edge, (y_block + 1) * block_edge)
            density = density_ref[x, span, :]
            fields[x + 1, 3, span, :] = factor * density * density
            fields[x + 1, 4, span, :] = density
    blank = jnp.zeros((rows - height, depth), jnp.float32)
    for x in range(width):
        for field in range(3):
            fields[x + 1, field, 0:height, :] = displacement_ref[field, x]
        for field in range(5):
            fields[x + 1, field, height:rows, :] = blank
    for x in range(width):
        for field in range(5):
            y_send[0, field, x : x + 1, :] = fields[x + 1, field, 0:1, :]
            y_send[1, field, x : x + 1, :] = fields[x + 1, field, height - 1 : height, :]

    def weigh(part, carry):
        span = pl.ds(pl.multiple_of(part * cap, lanes), cap)
        element = element_ref[:, span]
        along_x = quotient(element, height * depth)
        along_y = quotient(element - along_x * (height * depth), depth)
        along_z = element - along_x * (height * depth) - along_y * depth

        def weights(lowest, along, count):
            positions = lax.broadcasted_iota(jnp.int32, (count, cap), 0)
            upper = jnp.where(positions == lowest + 1, along, 0.0)
            return jnp.where(positions == lowest, 1.0 - along, upper)

        weight_x[:, span] = weights(along_x, coords_ref[0, :, span], width)
        weight_y[:, span] = weights(along_y, coords_ref[1, :, span], height)
        high, low = halves(weights(along_z, coords_ref[2, :, span], depth))
        weight_z[0:depth, span] = high
        weight_z[depth : 2 * depth, span] = low
        return carry

    lax.fori_loop(0, parts, weigh, 0)

    def barrier_count():
        return (
            parts
            - 1
            + jnp.where(column > 0, 1, 0)
            + jnp.where(column < columns - 1, 1, 0)
        )

    pl.semaphore_wait(barrier, barrier_count())

    def y_copy(side):
        return pltpu.make_async_remote_copy(
            src_ref=y_send.at[side],
            dst_ref=y_recv.at[1 - side],
            send_sem=y_sems.at[side],
            recv_sem=y_sems.at[3 - side],
            device_id=(me, column - 1 if side == 0 else column + 1),
            device_id_type=MESH,
        )

    def x_copy(side):
        return pltpu.make_async_remote_copy(
            src_ref=fields.at[1 if side == 0 else width],
            dst_ref=x_recv.at[1 - side],
            send_sem=x_sems.at[side],
            recv_sem=x_sems.at[3 - side],
            device_id=(me - 1 if side == 0 else me + 1, column),
            device_id_type=MESH,
        )

    y_there = (column > 0, column < columns - 1)
    x_there = (me > 0, me < parts - 1)
    for side in range(2):

        @pl.when(y_there[side])
        def _():
            y_copy(side).start()

    def slot_copy(source, target, send_sems, recv_sems, other, slot):
        return pltpu.make_async_remote_copy(
            src_ref=source.at[other],
            dst_ref=target.at[slot],
            send_sem=send_sems.at[other],
            recv_sem=recv_sems.at[slot],
            device_id=(other, column),
            device_id_type=MESH,
        )

    high, low = halves(displacement_ref[...].reshape(3 * width * height, depth))
    high = jnp.concatenate([high, high], axis=1)
    low = jnp.concatenate([low, low], axis=1)

    def planar_weights(span):
        planar = weight_x[:, span][:, None, :] * weight_y[:, span][None]
        return planar.reshape(width * height, cap)

    def interpolate(step, carry):
        other = lax.rem(me + step, parts)
        span = pl.ds(pl.multiple_of(other * cap, lanes), cap)
        weight = weight_z[:, span]
        sums = dot(high, weight) + dot(low, weight)
        planar = planar_weights(span)
        for field in range(3):
            piece = sums[field * width * height : (field + 1) * width * height]
            send_out[other, field : field + 1, :] = jnp.sum(piece * planar, axis=0, keepdims=True)

        @pl.when(other != me)
        def _():
            slot_copy(send_out, recv_out, out_send_sems, out_recv_sems, other, me).start()

        return carry

    lax.fori_loop(1, parts + 1, interpolate, 0)
    recv_out[me] = send_out[me]

    slots = jnp.concatenate([slot_ref[fibre] for fibre in range(fibres)], axis=1)
    slot_row = quotient(slots, lanes)
    slot_lane = slots - slot_row * lanes
    lane_count = lax.broadcasted_iota(jnp.int32, (lanes, slots.shape[1]), 0)
    onehot[...] = jnp.where(lane_count == slot_lane, 1.0, 0.0).astype(jnp.bfloat16)
    in_row = lax.broadcasted_iota(jnp.int32, (all_rows, slots.shape[1]), 0) == slot_row
    for fibre in range(fibres):
        for index in range(2):
            angles[index, fibre : fibre + 1, :] = angle_ref[index, fibre]
    azimuth, elevation = angles[0], angles[1]
    flat = jnp.cos(elevation)
    direction = (jnp.cos(azimuth) * flat, jnp.sin(azimuth) * flat, jnp.sin(elevation))

    for side in range(2):

        @pl.when(y_there[side])
        def _():
            y_copy(1 - side).wait_recv()

        @pl.when(jnp.logical_not(y_there[side]))
        def _():
            y_recv[side] = jnp.zeros(y_recv.shape[1:], jnp.float32)

    for x in range(width):
        for field in range(5):
            fields[x + 1, field, rows - 1 : rows, :] = y_recv[0, field, x : x + 1, :]
            fields[x + 1, field, height : height + 1, :] = y_recv[1, field, x : x + 1, :]
    for side in range(2):

        @pl.when(x_there[side])
        def _():
            x_copy(side).start()

    def await_out(step, carry):
        other = lax.rem(me + step, parts)
        slot_copy(send_out, recv_out, out_send_sems, out_recv_sems, other, other).wait_recv()
        return carry

    lax.fori_loop(1, parts, await_out, 0)

    for field in range(3):
        for part in range(parts):
            for row in range(slot_rows):
                place = field * all_rows + part * slot_rows + row
                picked[place : place + 1, :] = recv_out[
                    part, field : field + 1, row * lanes : (row + 1) * lanes
                ]
    near, rest = halves(picked[...])
    chosen = dot(near, onehot[...]) + dot(rest, onehot[...])
    segments = angles.shape[2]
    for field in range(3):
        piece = chosen[field * all_rows : (field + 1) * all_rows]
        line = jnp.sum(jnp.where(in_row, piece, 0.0), axis=0, keepdims=True)
        for fibre in range(fibres):
            nodes[field, fibre : fibre + 1, :] = line[:, fibre * segments : (fibre + 1) * segments]
    along = jnp.zeros((fibres, segments), jnp.float32)
    for field in range(3):
        place = nodes[field]
        along = along + direction[field] * (pltpu.roll(place, segments - 1, 1) - place)
    live = lax.broadcasted_iota(jnp.int32, along.shape, 1) < segments - 1
    tension = jnp.where(live, stiffness_ref[...] * jnp.maximum(along, 0.0), 0.0)
    terms = []
    for field in range(3):
        pull = tension * direction[field]
        nodes[field] = pull - pltpu.roll(pull, 1, 1)
        line = jnp.concatenate(
            [nodes[field, fibre : fibre + 1, :] for fibre in range(fibres)], axis=1
        )
        terms.append(jnp.where(in_row, line, 0.0))
    near, rest = halves(jnp.concatenate(terms, axis=0))
    picked[...] = dot_t(near, onehot[...]) + dot_t(rest, onehot[...])
    for field in range(3):
        for part in range(parts):
            for row in range(slot_rows):
                place = field * all_rows + part * slot_rows + row
                send_back[part, field : field + 1, row * lanes : (row + 1) * lanes] = picked[
                    place : place + 1, :
                ]

    def give_back(step, carry):
        other = lax.rem(me + step, parts)
        slot_copy(send_back, recv_back, back_send_sems, back_recv_sems, other, me).start()
        return carry

    lax.fori_loop(1, parts, give_back, 0)
    recv_back[me] = send_back[me]

    for side in range(2):
        edge = 0 if side == 0 else width + 1

        @pl.when(x_there[side])
        def _():
            x_copy(1 - side).wait_recv()
            fields[edge] = x_recv[side]

        @pl.when(jnp.logical_not(x_there[side]))
        def _():
            fields[edge] = jnp.zeros(fields.shape[1:], jnp.float32)

    table = mode_stiffness()
    level = lax.broadcasted_iota(jnp.int32, (rows, depth), 1)

    def plane_modes(plane):
        modes = []
        for field in range(3):
            value = fields[plane, field]
            above = jnp.where(level < depth - 1, pltpu.roll(value, depth - 1, 1), 0.0)
            pair = (value + above, above - value)
            beside = [pltpu.roll(item, rows - 1, 0) for item in pair]
            modes.append(
                [pair[0] + beside[0], pair[1] + beside[1], beside[0] - pair[0], beside[1] - pair[1]]
            )
        return modes

    def lift(value):
        return jnp.where(level > 0, pltpu.roll(value, 1, 1), 0.0)

    def layer(plane, carry):
        near_modes, far_modes = plane_modes(plane), plane_modes(plane + 1)
        modes = [None] * 24
        for field in range(3):
            for mode in range(4):
                low_side, high_side = near_modes[field][mode], far_modes[field][mode]
                modes[3 * mode + field] = high_side + low_side
                modes[3 * (mode + 4) + field] = high_side - low_side
        modulus = fields[plane, 3]
        forces = []
        for row in range(24):
            force = None
            for place in range(24):
                if table[row, place] != 0.0:
                    term = jnp.float32(table[row, place]) * modes[place]
                    force = term if force is None else force + term
            forces.append(None if force is None else force * modulus)
        passed = []
        for field in range(3):
            joined = []
            for mode in range(4):
                even, odd = forces[3 * mode + field], forces[3 * (mode + 4) + field]
                even = jnp.zeros_like(odd) if even is None else even
                joined.append(carry[4 * field + mode] + even - odd)
                passed.append(even + odd)
            flat_z = []
            for mode in range(2):
                even, odd = joined[mode], joined[mode + 2]
                flat_z.append(even - odd + pltpu.roll(even + odd, 1, 0))
            result = flat_z[0] - flat_z[1] + lift(flat_z[0] + flat_z[1])
            elastic[plane, field] = result[0:height]
        density = fields[plane, 4]
        density = density + pltpu.roll(density, 1, 0)
        density = density + lift(density)
        mass[plane] = 0.125 * (carry[12] + density)[0:height]
        return tuple(passed) + (density,)

    lax.fori_loop(
        0,
        width + 1,
        layer,
        tuple(jnp.zeros((rows, depth), jnp.float32) for _ in range(13)),
    )

    total[...] = jnp.zeros(total.shape, jnp.float32)

    def spread(step, carry):
        other = lax.rem(me + step, parts)

        @pl.when(other != me)
        def _():
            slot_copy(send_back, recv_back, back_send_sems, back_recv_sems, other, other).wait_recv()

        span = pl.ds(pl.multiple_of(other * cap, lanes), cap)
        force = recv_back[other]
        planar = planar_weights(span)
        near, rest = halves(
            jnp.concatenate([planar * force[field : field + 1] for field in range(3)], axis=0)
        )
        total[...] += dot_t(jnp.concatenate([near, rest], axis=0), weight_z[:, span])
        return carry

    lax.fori_loop(0, parts, spread, 0)
    count = 3 * width * height
    fibre = (
        total[0:count, 0:depth]
        + total[0:count, depth : 2 * depth]
        + total[count : 2 * count, 0:depth]
        + total[count : 2 * count, depth : 2 * depth]
    ).reshape(3, width, height, depth)
    weight = mass[1 : width + 1]
    for field in range(3):
        velocity = velocity_ref[field]
        acceleration = (
            load_ref[field] - elastic[1 : width + 1, field] + fibre[field]
        ) / weight - damping * velocity
        velocity = velocity + time_step * acceleration
        new_velocity_ref[field] = velocity
        new_displacement_ref[field] = displacement_ref[field] + time_step * velocity

    for side in range(2):

        @pl.when(y_there[side])
        def _():
            y_copy(side).wait_send()

        @pl.when(x_there[side])
        def _():
            x_copy(side).wait_send()

    def await_sends(step, carry):
        other = lax.rem(me + step, parts)
        slot_copy(send_out, recv_out, out_send_sems, out_recv_sems, other, me).wait_send()
        slot_copy(send_back, recv_back, back_send_sems, back_recv_sems, other, me).wait_send()
        return carry

    lax.fori_loop(1, parts, await_sends, 0)


def shards(
    displacement,
    velocity,
    load,
    density,
    block_class,
    host_element,
    host_coords,
    fibre_slot,
    fibre_angles,
    fibre_stiffness,
):
    _, width, height, depth = displacement.shape
    parts = lax.axis_size("dom")
    columns = lax.axis_size("blk")
    slots = host_element.shape[1]
    cap = slots // parts
    fibres, _, count = fibre_slot.shape
    rows = height + 8
    f32 = jnp.float32
    vmem = pl.BlockSpec(memory_space=pltpu.VMEM)
    boxes = pltpu.VMEM((parts, 3, cap), f32)
    return pl.pallas_call(
        functools.partial(kernel, parts, columns),
        out_shape=(
            jax.ShapeDtypeStruct(displacement.shape, f32),
            jax.ShapeDtypeStruct(displacement.shape, f32),
        ),
        in_specs=[pl.BlockSpec(memory_space=pltpu.SMEM)] + [vmem] * 9,
        out_specs=(vmem, vmem),
        scratch_shapes=[
            pltpu.VMEM((width + 2, 5, rows, depth), f32),
            pltpu.VMEM((2, 5, width, depth), f32),
            pltpu.VMEM((2, 5, width, depth), f32),
            pltpu.VMEM((2, 5, rows, depth), f32),
            pltpu.VMEM((2 * depth, slots), jnp.bfloat16),
            pltpu.VMEM((width, slots), f32),
            pltpu.VMEM((height, slots), f32),
            pltpu.VMEM((lanes, fibres * count), jnp.bfloat16),
            pltpu.VMEM((2, fibres, count), f32),
            pltpu.VMEM((3 * slots // lanes, lanes), f32),
            pltpu.VMEM((3, fibres, count), f32),
            boxes,
            boxes,
            boxes,
            boxes,
            pltpu.VMEM((6 * width * height, 2 * depth), f32),
            pltpu.VMEM((width + 1, 3, height, depth), f32),
            pltpu.VMEM((width + 1, height, depth), f32),
            pltpu.SemaphoreType.DMA((4,)),
            pltpu.SemaphoreType.DMA((4,)),
            pltpu.SemaphoreType.DMA((parts,)),
            pltpu.SemaphoreType.DMA((parts,)),
            pltpu.SemaphoreType.DMA((parts,)),
            pltpu.SemaphoreType.DMA((parts,)),
        ],
        compiler_params=pltpu.CompilerParams(
            collective_id=0, has_side_effects=True, vmem_limit_bytes=32 * 1024 * 1024
        ),
    )(
        block_class,
        displacement,
        velocity,
        load,
        density,
        host_element,
        host_coords,
        fibre_slot,
        fibre_angles,
        fibre_stiffness,
    )


def solution(mesh):
    return jax.shard_map(
        shards,
        mesh=mesh,
        in_specs=(
            P(None, "dom", "blk", None),
            P(None, "dom", "blk", None),
            P(None, "dom", "blk", None),
            P("dom", "blk", None),
            P("dom", "blk", None),
            P("blk", "dom"),
            P(None, "blk", "dom"),
            P("dom", "blk", None),
            P(None, "dom", "blk", None),
            P("dom", "blk"),
        ),
        out_specs=(P(None, "dom", "blk", None), P(None, "dom", "blk", None)),
        check_vma=False,
    )
```

time: 49.8 us -> 23.9 us (0.48)
  starting transfers between devices: 20.2 us -> 0 us
  matrix products: 16.1 us -> 0 us
  Pallas kernels: 0 us -> 15.1 us
  other arithmetic: 6.49 us -> 0 us
  local copies, waits for them, and re-layouts: 4.96 us -> 7.7 us
  between operations: 1.21 us -> 0.67 us
    dot_general x12 -> x0, matrix products: 16.1 us -> none  [the longest x8 8.33 us: element_forces(): jnp.einsum('ij,jxyz->ixyz', table[:, 3 * corner:3 * corner + 3], local, p...]
    pallas_call x0 -> x1, Pallas kernels: none -> 15.1 us  [shards(): pl.pallas_call(functools.partial(kernel, parts, columns), out_shape=(jax....]
    ppermute x4 -> x0, starting transfers between devices: 10.2 us -> none  [the longest x2 7.58 us: padded_2(): lax.ppermute(lax.slice_in_dim(block, block.shape[dim] - width, None, axis...]
    all_to_all x2 -> x0, starting transfers between devices: 9.99 us -> none  [the longest x1 5.79 us: shards(): lax.all_to_all(places.reshape(3, parts, -1), 'dom', split_axis=1, concat_...]
    unnamed x37 -> x21, local copies, waits for them, and re-layouts: 2.4 us -> 7.7 us
    add x5 -> x0, other arithmetic: 2.36 us -> none  [the longest x2 1.67 us: axis_weights(): lowest[None] + 1]
    slice x8 -> x0, local copies, waits for them, and re-layouts: 1.7 us -> none  [the longest x1 0.76 us: slot_weights(): weight_z = axis_weights(coords[2], along_z, depth)]
    reduce_sum x2 -> x0, other arithmetic: 1.11 us -> none  [the longest x1 1.03 us: interpolate(): jnp.sum(partial_sums.reshape(3, width * height, -1) * planar[None], axis=1)]
  transfers between devices with their start and end apart: 6 -> 0, of which waited for: 0 -> 0; matrix products, arithmetic and copies ran while one was open for 39% -> 0% of each run, Pallas kernels for 0% -> 0%
where the time goes in v2:
time: 23.9 us; the launch traced here: 23.5 us
  Pallas kernels  15.1 us (63%)
  local copies, waits for them, and re-layouts  7.7 us (32%)
  between operations  0.67 us (3%)
    pallas_call x1, Pallas kernels, shards(): pl.pallas_call(functools.partial(kernel, parts, columns), out_shape=(jax....  15.1 us
    unnamed x21, local copies, waits for them, and re-layouts  7.7 us

profile of v2, /device:TPU:0, one launch (start us, length us, event | category | flops | bytes accessed | tf_op | source)
XLA Modules:
  0.0 23.5 jit_solution(16701760696215528497)
XLA Ops:
  0.6 0.0 copy-start.7
  0.6 0.0 copy-start.8
  0.7 0.7 %copy.12.stiffness_ref = f32[16,1]{1,0:T(8,128)S(1)} copy(f32[16,1]{0,1:T(1,128)} %param.19) | data formatting | bytes 128 | tf_op args[9]
  1.4 0.0 copy-done.7
  1.4 0.0 copy-done.8
  1.4 0.0 copy-start
  1.4 0.9 %copy-done = f32[3,8,8,128]{3,2,1,0:T(8,128)S(1)} copy-done((f32[3,8,8,128]{3,2,1,0:T(8,128)S(1)}, f32[3,8,8,128]{3,2,1,0:T(8,128)}, u32[]{:S(2)}) %copy-start) | copy-done | bytes 98328
  2.3 0.0 copy-start.1
  2.3 0.9 %copy-done.1 = f32[3,8,8,128]{3,2,1,0:T(8,128)S(1)} copy-done((f32[3,8,8,128]{3,2,1,0:T(8,128)S(1)}, f32[3,8,8,128]{3,2,1,0:T(8,128)}, u32[]{:S(2)}) %copy-start.1) | copy-done | bytes 98328
  3.2 0.0 copy-start.2
  3.2 0.9 %copy-done.2 = f32[3,8,8,128]{3,2,1,0:T(8,128)S(1)} copy-done((f32[3,8,8,128]{3,2,1,0:T(8,128)S(1)}, f32[3,8,8,128]{3,2,1,0:T(8,128)}, u32[]{:S(2)}) %copy-start.2) | copy-done | bytes 98328
  4.1 0.0 copy-start.3
  4.1 0.8 %copy-done.3 = f32[3,1,4096]{2,1,0:T(1,128)S(1)} copy-done((f32[3,1,4096]{2,1,0:T(1,128)S(1)}, f32[3,1,4096]{2,1,0:T(1,128)}, u32[]{:S(2)}) %copy-start.3) | copy-done | bytes 49176
  4.9 0.0 copy-start.4
  4.9 0.8 %copy-done.4 = f32[8,8,128]{2,1,0:T(8,128)S(1)} copy-done((f32[8,8,128]{2,1,0:T(8,128)S(1)}, f32[8,8,128]{2,1,0:T(8,128)}, u32[]{:S(2)}) %copy-start.4) | copy-done | bytes 32792
  5.6 0.0 copy-start.5
  5.6 0.7 %copy-done.5 = s32[1,4096]{1,0:T(1,128)S(1)} copy-done((s32[1,4096]{1,0:T(1,128)S(1)}, s32[1,4096]{1,0:T(1,128)}, u32[]{:S(2)}) %copy-start.5) | copy-done | bytes 16408
  6.4 0.0 copy-start.6
  6.4 0.7 %copy-done.6 = f32[2,16,1,128]{3,2,1,0:T(1,128)S(1)} copy-done((f32[2,16,1,128]{3,2,1,0:T(1,128)S(1)}, f32[2,16,1,128]{3,2,1,0:T(1,128)}, u32[]{:S(2)}) %copy-start.6) | copy-done | bytes 16408
  7.1 15.1 %shard_map.113 = (f32[3,8,8,128]{3,2,1,0:T(8,128)S(1)}, f32[3,8,8,128]{3,2,1,0:T(8,128)S(1)}) custom-call(s32[1,1,16]{2,1,0:T(1,128)S(1)} %copy-done.8, f32[3,8,8,128]{3,2,1,0:T(8,128)S(1)} %copy-done, f32[3,8,8,128]{3,2,1,0:T(8,128)S(1)} %copy-done.1, f32[3,8,8,128]{3,2,1,0:T(8,128)S(1)} %copy-done.2, f32[8,8,128]{2,1,0:T(8,128)S(1)} %copy-done.4, ...), custom_call_target="tpu_custom_call" | custom-call | tf_op jit(solution)/shard_map/pallas_call | solution.py:511
  22.2 0.6 %copy.15 = f32[3,8,8,128]{3,2,1,0:T(8,128)} copy(f32[3,8,8,128]{3,2,1,0:T(8,128)S(1)} %get-tuple-element.4) | data formatting | bytes 196608
  22.8 0.6 %copy.16 = f32[3,8,8,128]{3,2,1,0:T(8,128)} copy(f32[3,8,8,128]{3,2,1,0:T(8,128)S(1)} %get-tuple-element.5) | data formatting | bytes 196608
Async XLA Ops:
  0.6 0.8 %copy-start.7 = (s32[16,1,128]{2,1,0:T(1,128)S(1)}, s32[16,1,128]{2,1,0:T(1,128)}, u32[]{:S(2)}) copy-start(s32[16,1,128]{2,1,0:T(1,128)} %slot_ref.1) | copy-start | bytes 24580
  0.6 0.8 %copy-start.8 = (s32[1,1,16]{2,1,0:T(1,128)S(1)}, s32[1,1,16]{2,1,0:T(1,128)}, u32[]{:S(2)}) copy-start(s32[1,1,16]{2,1,0:T(1,128)} %class_ref.1) | copy-start | bytes 196
  1.4 0.9 %copy-start = (f32[3,8,8,128]{3,2,1,0:T(8,128)S(1)}, f32[3,8,8,128]{3,2,1,0:T(8,128)}, u32[]{:S(2)}) copy-start(f32[3,8,8,128]{3,2,1,0:T(8,128)} %displacement_ref.1) | copy-start | bytes 294916
  2.3 0.9 %copy-start.1 = (f32[3,8,8,128]{3,2,1,0:T(8,128)S(1)}, f32[3,8,8,128]{3,2,1,0:T(8,128)}, u32[]{:S(2)}) copy-start(f32[3,8,8,128]{3,2,1,0:T(8,128)} %velocity_ref.1) | copy-start | bytes 294916
  3.2 0.9 %copy-start.2 = (f32[3,8,8,128]{3,2,1,0:T(8,128)S(1)}, f32[3,8,8,128]{3,2,1,0:T(8,128)}, u32[]{:S(2)}) copy-start(f32[3,8,8,128]{3,2,1,0:T(8,128)} %load_ref.1) | copy-start | bytes 294916
  4.1 0.8 %copy-start.3 = (f32[3,1,4096]{2,1,0:T(1,128)S(1)}, f32[3,1,4096]{2,1,0:T(1,128)}, u32[]{:S(2)}) copy-start(f32[3,1,4096]{2,1,0:T(1,128)} %coords_ref.1) | copy-start | bytes 147460
  4.9 0.8 %copy-start.4 = (f32[8,8,128]{2,1,0:T(8,128)S(1)}, f32[8,8,128]{2,1,0:T(8,128)}, u32[]{:S(2)}) copy-start(f32[8,8,128]{2,1,0:T(8,128)} %density_ref.1) | copy-start | bytes 98308
  5.6 0.7 %copy-start.5 = (s32[1,4096]{1,0:T(1,128)S(1)}, s32[1,4096]{1,0:T(1,128)}, u32[]{:S(2)}) copy-start(s32[1,4096]{1,0:T(1,128)} %element_ref.1) | copy-start | bytes 49156
  6.4 0.7 %copy-start.6 = (f32[2,16,1,128]{3,2,1,0:T(1,128)S(1)}, f32[2,16,1,128]{3,2,1,0:T(1,128)}, u32[]{:S(2)}) copy-start(f32[2,16,1,128]{3,2,1,0:T(1,128)} %angle_ref.1) | copy-start | bytes 49156

commit v3 on v2

--- a/solution.py
+++ b/solution.py
@@ -13,6 +13,17 @@
 damping = 0.5
 block_edge = 8
 lanes = 128
+operand_order = (
+    "displacement",
+    "density",
+    "class",
+    "element",
+    "coords",
+    "slot",
+    "angle",
+    "stiffness",
+    "load",
+)
 MESH = pl.DeviceIdType.MESH
 
 
@@ -85,18 +96,21 @@
 def kernel(
     parts,
     columns,
-    class_ref,
-    displacement_ref,
-    velocity_ref,
-    load_ref,
-    density_ref,
-    element_ref,
-    coords_ref,
-    slot_ref,
-    angle_ref,
-    stiffness_ref,
-    new_displacement_ref,
-    new_velocity_ref,
+    *refs,
+):
+    names = len(operand_order)
+    sources, ratio_ref, buffers = refs[:names], refs[names], refs[names + 1 :]
+    local = dict(zip(operand_order, buffers[:names]))
+    step_kernel(parts, columns, sources, local, ratio_ref, *buffers[names:])
+
+
+def step_kernel(
+    parts,
+    columns,
+    sources,
+    local,
+    ratio_ref,
+    in_sems,
     fields,
     y_send,
     y_recv,
@@ -122,6 +136,17 @@
     back_send_sems,
     back_recv_sems,
 ):
+    copies = {}
+    for index, name in enumerate(operand_order):
+        copies[name] = pltpu.make_async_copy(sources[index], local[name], in_sems.at[index])
+        copies[name].start()
+    displacement_ref, load_ref, density_ref = (
+        local["displacement"],
+        local["load"],
+        local["density"],
+    )
+    class_ref, element_ref, coords_ref = local["class"], local["element"], local["coords"]
+    slot_ref, angle_ref, stiffness_ref = local["slot"], local["angle"], local["stiffness"]
     _, width, height, depth = displacement_ref.shape
     rows = fields.shape[2]
     cap = recv_out.shape[2]
@@ -148,21 +173,24 @@
     def _():
         pl.semaphore_signal(barrier, inc=1, device_id=(me, column + 1), device_id_type=MESH)
 
+    for name in ("displacement", "density", "class"):
+        copies[name].wait()
+
     block_of = quotient(lax.broadcasted_iota(jnp.int32, (1, depth), 1), block_edge)
-    for x in range(width):
+    for x_block in range(width // block_edge):
         for y_block in range(height // block_edge):
+            kinds = class_ref[x_block, y_block : y_block + 1, :]
             classes = jnp.zeros((1, depth), jnp.int32)
             for z_block in range(depth // block_edge):
-                classes = jnp.where(
-                    block_of == z_block, class_ref[x // block_edge, y_block, z_block], classes
-                )
+                classes = jnp.where(block_of == z_block, kinds[:, z_block : z_block + 1], classes)
             factor = jnp.zeros((1, depth), jnp.float32)
             for index, value in enumerate(class_values):
                 factor = jnp.where(classes == index, jnp.float32(value), factor)
             span = slice(y_block * block_edge, (y_block + 1) * block_edge)
-            density = density_ref[x, span, :]
-            fields[x + 1, 3, span, :] = factor * density * density
-            fields[x + 1, 4, span, :] = density
+            for x in range(x_block * block_edge, (x_block + 1) * block_edge):
+                density = density_ref[x, span, :]
+                fields[x + 1, 3, span, :] = factor * density * density
+                fields[x + 1, 4, span, :] = density
     blank = jnp.zeros((rows - height, depth), jnp.float32)
     for x in range(width):
         for field in range(3):
@@ -174,6 +202,9 @@
             y_send[0, field, x : x + 1, :] = fields[x + 1, field, 0:1, :]
             y_send[1, field, x : x + 1, :] = fields[x + 1, field, height - 1 : height, :]
 
+    for name in ("element", "coords"):
+        copies[name].wait()
+
     def weigh(part, carry):
         span = pl.ds(pl.multiple_of(part * cap, lanes), cap)
         element = element_ref[:, span]
@@ -244,8 +275,9 @@
         )
 
     high, low = halves(displacement_ref[...].reshape(3 * width * height, depth))
-    high = jnp.concatenate([high, high], axis=1)
-    low = jnp.concatenate([low, low], axis=1)
+    count = 3 * width * height
+    both = jnp.concatenate([high, low], axis=0)
+    both = jnp.concatenate([both, both], axis=1)
 
     def planar_weights(span):
         planar = weight_x[:, span][:, None, :] * weight_y[:, span][None]
@@ -254,8 +286,8 @@
     def interpolate(step, carry):
         other = lax.rem(me + step, parts)
         span = pl.ds(pl.multiple_of(other * cap, lanes), cap)
-        weight = weight_z[:, span]
-        sums = dot(high, weight) + dot(low, weight)
+        sums = dot(both, weight_z[:, span])
+        sums = sums[:count] + sums[count:]
         planar = planar_weights(span)
         for field in range(3):
             piece = sums[field * width * height : (field + 1) * width * height]
@@ -270,6 +302,12 @@
     lax.fori_loop(1, parts + 1, interpolate, 0)
     recv_out[me] = send_out[me]
 
+    for name in ("slot", "angle", "stiffness", "load"):
+        copies[name].wait()
+    diagonal = lax.broadcasted_iota(jnp.int32, (fibres, fibres), 0) == lax.broadcasted_iota(
+        jnp.int32, (fibres, fibres), 1
+    )
+    stiffness = jnp.sum(jnp.where(diagonal, stiffness_ref[...], 0.0), axis=1, keepdims=True)
     slots = jnp.concatenate([slot_ref[fibre] for fibre in range(fibres)], axis=1)
     slot_row = quotient(slots, lanes)
     slot_lane = slots - slot_row * lanes
@@ -318,7 +356,8 @@
                     part, field : field + 1, row * lanes : (row + 1) * lanes
                 ]
     near, rest = halves(picked[...])
-    chosen = dot(near, onehot[...]) + dot(rest, onehot[...])
+    chosen = dot(jnp.concatenate([near, rest], axis=0), onehot[...])
+    chosen = chosen[: 3 * all_rows] + chosen[3 * all_rows :]
     segments = angles.shape[2]
     for field in range(3):
         piece = chosen[field * all_rows : (field + 1) * all_rows]
@@ -330,7 +369,7 @@
         place = nodes[field]
         along = along + direction[field] * (pltpu.roll(place, segments - 1, 1) - place)
     live = lax.broadcasted_iota(jnp.int32, along.shape, 1) < segments - 1
-    tension = jnp.where(live, stiffness_ref[...] * jnp.maximum(along, 0.0), 0.0)
+    tension = jnp.where(live, stiffness * jnp.maximum(along, 0.0), 0.0)
     terms = []
     for field in range(3):
         pull = tension * direction[field]
@@ -340,7 +379,8 @@
         )
         terms.append(jnp.where(in_row, line, 0.0))
     near, rest = halves(jnp.concatenate(terms, axis=0))
-    picked[...] = dot_t(near, onehot[...]) + dot_t(rest, onehot[...])
+    sums = dot_t(jnp.concatenate([near, rest], axis=0), onehot[...])
+    picked[...] = sums[: 3 * all_rows] + sums[3 * all_rows :]
     for field in range(3):
         for part in range(parts):
             for row in range(slot_rows):
@@ -450,7 +490,6 @@
         return carry
 
     lax.fori_loop(0, parts, spread, 0)
-    count = 3 * width * height
     fibre = (
         total[0:count, 0:depth]
         + total[0:count, depth : 2 * depth]
@@ -459,13 +498,9 @@
     ).reshape(3, width, height, depth)
     weight = mass[1 : width + 1]
     for field in range(3):
-        velocity = velocity_ref[field]
-        acceleration = (
+        ratio_ref[field] = (
             load_ref[field] - elastic[1 : width + 1, field] + fibre[field]
-        ) / weight - damping * velocity
-        velocity = velocity + time_step * acceleration
-        new_velocity_ref[field] = velocity
-        new_displacement_ref[field] = displacement_ref[field] + time_step * velocity
+        ) / weight
 
     for side in range(2):
 
@@ -508,15 +543,25 @@
     f32 = jnp.float32
     vmem = pl.BlockSpec(memory_space=pltpu.VMEM)
     boxes = pltpu.VMEM((parts, 3, cap), f32)
-    return pl.pallas_call(
+    operands = (
+        displacement,
+        density,
+        block_class,
+        host_element,
+        host_coords,
+        fibre_slot,
+        fibre_angles,
+        fibre_stiffness.reshape(1, fibres),
+        load,
+    )
+    ratio = pl.pallas_call(
         functools.partial(kernel, parts, columns),
-        out_shape=(
-            jax.ShapeDtypeStruct(displacement.shape, f32),
-            jax.ShapeDtypeStruct(displacement.shape, f32),
-        ),
-        in_specs=[pl.BlockSpec(memory_space=pltpu.SMEM)] + [vmem] * 9,
-        out_specs=(vmem, vmem),
-        scratch_shapes=[
+        out_shape=jax.ShapeDtypeStruct(displacement.shape, f32),
+        in_specs=[pl.BlockSpec(memory_space=pltpu.HBM)] * len(operands),
+        out_specs=vmem,
+        scratch_shapes=[pltpu.VMEM(operand.shape, operand.dtype) for operand in operands]
+        + [
+            pltpu.SemaphoreType.DMA((len(operands),)),
             pltpu.VMEM((width + 2, 5, rows, depth), f32),
             pltpu.VMEM((2, 5, width, depth), f32),
             pltpu.VMEM((2, 5, width, depth), f32),
@@ -545,18 +590,9 @@
         compiler_params=pltpu.CompilerParams(
             collective_id=0, has_side_effects=True, vmem_limit_bytes=32 * 1024 * 1024
         ),
-    )(
-        block_class,
-        displacement,
-        velocity,
-        load,
-        density,
-        host_element,
-        host_coords,
-        fibre_slot,
-        fibre_angles,
-        fibre_stiffness,
-    )
+    )(*operands)
+    new_velocity = velocity + time_step * (ratio - damping * velocity)
+    return displacement + time_step * new_velocity, new_velocity
 
 
 def solution(mesh):

time: 23.9 us -> 23 us (0.962)
  local copies, waits for them, and re-layouts: 7.7 us -> 6.13 us
  other arithmetic: 0 us -> 0.7 us
    unnamed x21 -> x20, local copies, waits for them, and re-layouts: 7.7 us -> 6.13 us
    add x0 -> x1, other arithmetic: none -> 0.7 us  [shards(): return (displacement + time_step * new_velocity, new_velocity)]
where the time goes in v3:
time: 23 us; the launch traced here: 22.6 us
  Pallas kernels  15.1 us (66%)
  local copies, waits for them, and re-layouts  6.13 us (27%)
  other arithmetic  0.7 us (3%)
  between operations  0.67 us (3%)
    pallas_call x1, Pallas kernels, shards(): pl.pallas_call(functools.partial(kernel, parts, columns), out_shape=jax.S...  15.1 us
    unnamed x20, local copies, waits for them, and re-layouts  6.13 us
    add x1, other arithmetic, shards(): return (displacement + time_step * new_velocity, new_velocity)  0.7 us

profile of v3, /device:TPU:0, one launch (start us, length us, event | category | flops | bytes accessed | tf_op | source)
XLA Modules:
  0.0 22.6 jit_solution(6097466962470805642)
XLA Ops:
  0.6 0.0 copy-start.8
  0.6 0.0 copy-start.7
  0.7 0.6 %copy-done.8 = f32[16,1]{0,1:T(1,128)S(1)} copy-done((f32[16,1]{0,1:T(1,128)S(1)}, f32[16,1]{0,1:T(1,128)}, u32[]{:S(2)}) %copy-start.8) | copy-done | bytes 88
  1.3 0.0 copy-done.7
  1.3 0.0 copy-start
  1.3 0.9 %copy-done = f32[3,8,8,128]{3,2,1,0:T(8,128)S(1)} copy-done((f32[3,8,8,128]{3,2,1,0:T(8,128)S(1)}, f32[3,8,8,128]{3,2,1,0:T(8,128)}, u32[]{:S(2)}) %copy-start) | copy-done | bytes 98328
  2.2 0.0 copy-start.1
  2.2 0.9 %copy-done.1 = f32[3,8,8,128]{3,2,1,0:T(8,128)S(1)} copy-done((f32[3,8,8,128]{3,2,1,0:T(8,128)S(1)}, f32[3,8,8,128]{3,2,1,0:T(8,128)}, u32[]{:S(2)}) %copy-start.1) | copy-done | bytes 98328
  3.1 0.0 copy-start.2
  3.1 0.8 %copy-done.2 = f32[3,1,4096]{2,1,0:T(1,128)S(1)} copy-done((f32[3,1,4096]{2,1,0:T(1,128)S(1)}, f32[3,1,4096]{2,1,0:T(1,128)}, u32[]{:S(2)}) %copy-start.2) | copy-done | bytes 49176
  3.9 0.0 copy-start.3
  3.9 0.8 %copy-done.3 = f32[8,8,128]{2,1,0:T(8,128)S(1)} copy-done((f32[8,8,128]{2,1,0:T(8,128)S(1)}, f32[8,8,128]{2,1,0:T(8,128)}, u32[]{:S(2)}) %copy-start.3) | copy-done | bytes 32792
  4.6 0.0 copy-start.4
  4.7 0.7 %copy-done.4 = s32[1,4096]{1,0:T(1,128)S(1)} copy-done((s32[1,4096]{1,0:T(1,128)S(1)}, s32[1,4096]{1,0:T(1,128)}, u32[]{:S(2)}) %copy-start.4) | copy-done | bytes 16408
  5.4 0.0 copy-start.5
  5.4 0.7 %copy-done.5 = f32[2,16,1,128]{3,2,1,0:T(1,128)S(1)} copy-done((f32[2,16,1,128]{3,2,1,0:T(1,128)S(1)}, f32[2,16,1,128]{3,2,1,0:T(1,128)}, u32[]{:S(2)}) %copy-start.5) | copy-done | bytes 16408
  6.1 0.0 copy-start.6
  6.1 0.7 %copy-done.6 = s32[16,1,128]{2,1,0:T(1,128)S(1)} copy-done((s32[16,1,128]{2,1,0:T(1,128)S(1)}, s32[16,1,128]{2,1,0:T(1,128)}, u32[]{:S(2)}) %copy-start.6) | copy-done | bytes 8216
  6.8 0.0 copy-start.9
  6.8 15.1 %shard_map.113 = f32[3,8,8,128]{3,2,1,0:T(8,128)S(1)} custom-call(f32[3,8,8,128]{3,2,1,0:T(8,128)S(1)} %copy-done, f32[8,8,128]{2,1,0:T(8,128)S(1)} %copy-done.3, s32[1,1,16]{2,1,0:T(1,128)S(1)} %copy-done.7, s32[1,4096]{1,0:T(1,128)S(1)} %copy-done.4, f32[3,1,4096]{2,1,0:T(1,128)S(1)} %copy-done.2, s32[16,1,128]{2,1,0:T(1,128)S(1)} %copy-done.6, ...), custom_call_target="tpu_custom_call" | custom-call | tf_op jit(solution)/shard_map/pallas_call | solution.py:557
  21.9 0.0 copy-done.9
  21.9 0.7 %multiply_add_fusion = (f32[3,8,8,128]{3,2,1,0:T(8,128)}, f32[3,8,8,128]{3,2,1,0:T(8,128)}) fusion(f32[3,8,8,128]{3,2,1,0:T(8,128)S(1)} %copy-done, f32[3,8,8,128]{3,2,1,0:T(8,128)S(1)} %copy-done.9, f32[3,8,8,128]{3,2,1,0:T(8,128)S(1)} %shard_map.113), kind=kLoop, calls=%fused_computation | loop fusion | flops 147456 | bytes 491520 | tf_op jit(solution)/shard_map/add | solution.py:595
Async XLA Ops:
  0.6 0.7 %copy-start.8 = (f32[16,1]{0,1:T(1,128)S(1)}, f32[16,1]{0,1:T(1,128)}, u32[]{:S(2)}) copy-start(f32[16,1]{0,1:T(1,128)} %param.19) | copy-start | bytes 196
  0.6 0.7 %copy-start.7 = (s32[1,1,16]{2,1,0:T(1,128)S(1)}, s32[1,1,16]{2,1,0:T(1,128)}, u32[]{:S(2)}) copy-start(s32[1,1,16]{2,1,0:T(1,128)} %refs_2_.1) | copy-start | bytes 196
  1.3 0.9 %copy-start = (f32[3,8,8,128]{3,2,1,0:T(8,128)S(1)}, f32[3,8,8,128]{3,2,1,0:T(8,128)}, u32[]{:S(2)}) copy-start(f32[3,8,8,128]{3,2,1,0:T(8,128)} %refs_0_.1) | copy-start | bytes 294916
  2.2 0.9 %copy-start.1 = (f32[3,8,8,128]{3,2,1,0:T(8,128)S(1)}, f32[3,8,8,128]{3,2,1,0:T(8,128)}, u32[]{:S(2)}) copy-start(f32[3,8,8,128]{3,2,1,0:T(8,128)} %refs_8_.1) | copy-start | bytes 294916
  3.1 0.8 %copy-start.2 = (f32[3,1,4096]{2,1,0:T(1,128)S(1)}, f32[3,1,4096]{2,1,0:T(1,128)}, u32[]{:S(2)}) copy-start(f32[3,1,4096]{2,1,0:T(1,128)} %refs_4_.1) | copy-start | bytes 147460
  3.9 0.8 %copy-start.3 = (f32[8,8,128]{2,1,0:T(8,128)S(1)}, f32[8,8,128]{2,1,0:T(8,128)}, u32[]{:S(2)}) copy-start(f32[8,8,128]{2,1,0:T(8,128)} %refs_1_.1) | copy-start | bytes 98308
  4.6 0.7 %copy-start.4 = (s32[1,4096]{1,0:T(1,128)S(1)}, s32[1,4096]{1,0:T(1,128)}, u32[]{:S(2)}) copy-start(s32[1,4096]{1,0:T(1,128)} %refs_3_.1) | copy-start | bytes 49156
  5.4 0.7 %copy-start.5 = (f32[2,16,1,128]{3,2,1,0:T(1,128)S(1)}, f32[2,16,1,128]{3,2,1,0:T(1,128)}, u32[]{:S(2)}) copy-start(f32[2,16,1,128]{3,2,1,0:T(1,128)} %refs_6_.1) | copy-start | bytes 49156
  6.1 0.7 %copy-start.6 = (s32[16,1,128]{2,1,0:T(1,128)S(1)}, s32[16,1,128]{2,1,0:T(1,128)}, u32[]{:S(2)}) copy-start(s32[16,1,128]{2,1,0:T(1,128)} %refs_5_.1) | copy-start | bytes 24580
  6.8 15.1 %copy-start.9 = (f32[3,8,8,128]{3,2,1,0:T(8,128)S(1)}, f32[3,8,8,128]{3,2,1,0:T(8,128)}, u32[]{:S(2)}) copy-start(f32[3,8,8,128]{3,2,1,0:T(8,128)} %param.11) | copy-start | bytes 294916

commit v4 on v3

--- a/solution.py
+++ b/solution.py
@@ -588,7 +588,7 @@
             pltpu.SemaphoreType.DMA((parts,)),
         ],
         compiler_params=pltpu.CompilerParams(
-            collective_id=0, has_side_effects=True, vmem_limit_bytes=32 * 1024 * 1024
+            collective_id=0, has_side_effects=True, vmem_limit_bytes=60 * 1024 * 1024
         ),
     )(*operands)
     new_velocity = velocity + time_step * (ratio - damping * velocity)

time: 23 us -> 18 us (0.78)
  local copies, waits for them, and re-layouts: 6.13 us -> 0.01 us
  other arithmetic: 0.7 us -> 1.59 us
  Pallas kernels: 15.1 us -> 15.5 us
    unnamed x20 -> x4, local copies, waits for them, and re-layouts: 6.13 us -> 0.01 us
    add x1, other arithmetic: 0.7 us -> 1.59 us  [shards(): return (displacement + time_step * new_velocity, new_velocity)]
    pallas_call x1, Pallas kernels: 15.1 us -> 15.5 us  [shards(): pl.pallas_call(functools.partial(kernel, parts, columns), out_shape=jax.S...]
where the time goes in v4:
time: 18 us; the launch traced here: 17.7 us
  Pallas kernels  15.5 us (86%)
  other arithmetic  1.59 us (9%)
  between operations  0.67 us (4%)
    pallas_call x1, Pallas kernels, shards(): pl.pallas_call(functools.partial(kernel, parts, columns), out_shape=jax.S...  15.5 us
    add x1, other arithmetic, shards(): return (displacement + time_step * new_velocity, new_velocity)  1.59 us

profile of v4, /device:TPU:0, one launch (start us, length us, event | category | flops | bytes accessed | tf_op | source)
XLA Modules:
  0.0 17.7 jit_solution(1908603595220564355)
XLA Ops:
  0.6 0.0 copy-start
  0.6 0.0 copy-start.1
  0.7 15.5 %shard_map.113 = f32[3,8,8,128]{3,2,1,0:T(8,128)} custom-call(f32[3,8,8,128]{3,2,1,0:T(8,128)} %refs_0_.1, f32[8,8,128]{2,1,0:T(8,128)} %refs_1_.1, s32[1,1,16]{2,1,0:T(1,128)} %refs_2_.1, s32[1,4096]{1,0:T(1,128)} %refs_3_.1, f32[3,1,4096]{2,1,0:T(1,128)} %refs_4_.1, s32[16,1,128]{2,1,0:T(1,128)} %refs_5_.1, f32[2,16,1,128]{3,2,1,0:T(1,128)} %refs_6_.1, ...), custom_call_target="tpu_custom_call" | custom-call | tf_op jit(solution)/shard_map/pallas_call | solution.py:557
  16.1 0.0 copy-done
  16.1 0.0 copy-done.1
  16.1 1.6 %multiply_add_fusion = (f32[3,8,8,128]{3,2,1,0:T(8,128)}, f32[3,8,8,128]{3,2,1,0:T(8,128)}) fusion(f32[3,8,8,128]{3,2,1,0:T(8,128)S(1)} %copy-done, f32[3,8,8,128]{3,2,1,0:T(8,128)S(1)} %copy-done.1, f32[3,8,8,128]{3,2,1,0:T(8,128)} %shard_map.113), kind=kLoop, calls=%fused_computation | loop fusion | flops 147456 | bytes 491520 | tf_op jit(solution)/shard_map/add | solution.py:595
Async XLA Ops:
  0.6 15.5 %copy-start = (f32[3,8,8,128]{3,2,1,0:T(8,128)S(1)}, f32[3,8,8,128]{3,2,1,0:T(8,128)}, u32[]{:S(2)}) copy-start(f32[3,8,8,128]{3,2,1,0:T(8,128)} %refs_0_.1) | copy-start | bytes 294916
  0.6 15.5 %copy-start.1 = (f32[3,8,8,128]{3,2,1,0:T(8,128)S(1)}, f32[3,8,8,128]{3,2,1,0:T(8,128)}, u32[]{:S(2)}) copy-start(f32[3,8,8,128]{3,2,1,0:T(8,128)} %param.11) | copy-start | bytes 294916

commit v5 on v4

--- a/solution.py
+++ b/solution.py
@@ -205,8 +205,7 @@
     for name in ("element", "coords"):
         copies[name].wait()
 
-    def weigh(part, carry):
-        span = pl.ds(pl.multiple_of(part * cap, lanes), cap)
+    def weigh(span):
         element = element_ref[:, span]
         along_x = quotient(element, height * depth)
         along_y = quotient(element - along_x * (height * depth), depth)
@@ -217,14 +216,15 @@
             upper = jnp.where(positions == lowest + 1, along, 0.0)
             return jnp.where(positions == lowest, 1.0 - along, upper)
 
-        weight_x[:, span] = weights(along_x, coords_ref[0, :, span], width)
-        weight_y[:, span] = weights(along_y, coords_ref[1, :, span], height)
+        across_x = weights(along_x, coords_ref[0, :, span], width)
+        across_y = weights(along_y, coords_ref[1, :, span], height)
         high, low = halves(weights(along_z, coords_ref[2, :, span], depth))
+        weight_x[:, span] = across_x
+        weight_y[:, span] = across_y
         weight_z[0:depth, span] = high
         weight_z[depth : 2 * depth, span] = low
-        return carry
-
-    lax.fori_loop(0, parts, weigh, 0)
+        planar = (across_x[:, None, :] * across_y[None]).reshape(width * height, cap)
+        return planar, jnp.concatenate([high, low], axis=0)
 
     def barrier_count():
         return (
@@ -283,23 +283,24 @@
         planar = weight_x[:, span][:, None, :] * weight_y[:, span][None]
         return planar.reshape(width * height, cap)
 
-    def interpolate(step, carry):
-        other = lax.rem(me + step, parts)
+    def interpolate(other):
         span = pl.ds(pl.multiple_of(other * cap, lanes), cap)
-        sums = dot(both, weight_z[:, span])
+        planar, weight = weigh(span)
+        sums = dot(both, weight)
         sums = sums[:count] + sums[count:]
-        planar = planar_weights(span)
         for field in range(3):
             piece = sums[field * width * height : (field + 1) * width * height]
             send_out[other, field : field + 1, :] = jnp.sum(piece * planar, axis=0, keepdims=True)
 
-        @pl.when(other != me)
-        def _():
-            slot_copy(send_out, recv_out, out_send_sems, out_recv_sems, other, me).start()
-
+    def hand_out(step, carry):
+        other = lax.rem(me + step, parts)
+        interpolate(other)
+        slot_copy(send_out, recv_out, out_send_sems, out_recv_sems, other, me).start()
         return carry
 
-    lax.fori_loop(1, parts + 1, interpolate, 0)
+    unroll = parts - 1 if parts <= 8 else 1
+    lax.fori_loop(1, parts, hand_out, 0, unroll=unroll)
+    interpolate(me)
     recv_out[me] = send_out[me]
 
     for name in ("slot", "angle", "stiffness", "load"):
@@ -471,25 +472,24 @@
         tuple(jnp.zeros((rows, depth), jnp.float32) for _ in range(13)),
     )
 
-    total[...] = jnp.zeros(total.shape, jnp.float32)
-
-    def spread(step, carry):
-        other = lax.rem(me + step, parts)
-
-        @pl.when(other != me)
-        def _():
-            slot_copy(send_back, recv_back, back_send_sems, back_recv_sems, other, other).wait_recv()
-
+
+    def spread(other):
         span = pl.ds(pl.multiple_of(other * cap, lanes), cap)
         force = recv_back[other]
         planar = planar_weights(span)
         near, rest = halves(
             jnp.concatenate([planar * force[field : field + 1] for field in range(3)], axis=0)
         )
-        total[...] += dot_t(jnp.concatenate([near, rest], axis=0), weight_z[:, span])
+        return dot_t(jnp.concatenate([near, rest], axis=0), weight_z[:, span])
+
+    def take_back(step, carry):
+        other = lax.rem(me + step, parts)
+        slot_copy(send_back, recv_back, back_send_sems, back_recv_sems, other, other).wait_recv()
+        total[...] += spread(other)
         return carry
 
-    lax.fori_loop(0, parts, spread, 0)
+    total[...] = spread(me)
+    lax.fori_loop(1, parts, take_back, 0, unroll=unroll)
     fibre = (
         total[0:count, 0:depth]
         + total[0:count, depth : 2 * depth]

time: 18 us -> 18.3 us (1.017)
  Pallas kernels: 15.5 us -> 15.8 us
    pallas_call x1, Pallas kernels: 15.5 us -> 15.8 us  [shards(): pl.pallas_call(functools.partial(kernel, parts, columns), out_shape=jax.S...]
where the time goes in v5:
time: 18.3 us; the launch traced here: 18.1 us
  Pallas kernels  15.8 us (86%)
  other arithmetic  1.59 us (9%)
  between operations  0.67 us (4%)
    pallas_call x1, Pallas kernels, shards(): pl.pallas_call(functools.partial(kernel, parts, columns), out_shape=jax.S...  15.8 us
    add x1, other arithmetic, shards(): return (displacement + time_step * new_velocity, new_velocity)  1.59 us

profile of v5, /device:TPU:0, one launch (start us, length us, event | category | flops | bytes accessed | tf_op | source)
XLA Modules:
  0.0 18.1 jit_solution(13310642953207402984)
XLA Ops:
  0.6 0.0 copy-start
  0.6 0.0 copy-start.1
  0.7 15.8 %shard_map.113 = f32[3,8,8,128]{3,2,1,0:T(8,128)} custom-call(f32[3,8,8,128]{3,2,1,0:T(8,128)} %refs_0_.1, f32[8,8,128]{2,1,0:T(8,128)} %refs_1_.1, s32[1,1,16]{2,1,0:T(1,128)} %refs_2_.1, s32[1,4096]{1,0:T(1,128)} %refs_3_.1, f32[3,1,4096]{2,1,0:T(1,128)} %refs_4_.1, s32[16,1,128]{2,1,0:T(1,128)} %refs_5_.1, f32[2,16,1,128]{3,2,1,0:T(1,128)} %refs_6_.1, ...), custom_call_target="tpu_custom_call" | custom-call | tf_op jit(solution)/shard_map/pallas_call | solution.py:557
  16.5 0.0 copy-done
  16.5 0.0 copy-done.1
  16.5 1.6 %multiply_add_fusion = (f32[3,8,8,128]{3,2,1,0:T(8,128)}, f32[3,8,8,128]{3,2,1,0:T(8,128)}) fusion(f32[3,8,8,128]{3,2,1,0:T(8,128)S(1)} %copy-done, f32[3,8,8,128]{3,2,1,0:T(8,128)S(1)} %copy-done.1, f32[3,8,8,128]{3,2,1,0:T(8,128)} %shard_map.113), kind=kLoop, calls=%fused_computation | loop fusion | flops 147456 | bytes 491520 | tf_op jit(solution)/shard_map/add | solution.py:595
Async XLA Ops:
  0.6 15.8 %copy-start = (f32[3,8,8,128]{3,2,1,0:T(8,128)S(1)}, f32[3,8,8,128]{3,2,1,0:T(8,128)}, u32[]{:S(2)}) copy-start(f32[3,8,8,128]{3,2,1,0:T(8,128)} %refs_0_.1) | copy-start | bytes 294916
  0.6 15.8 %copy-start.1 = (f32[3,8,8,128]{3,2,1,0:T(8,128)S(1)}, f32[3,8,8,128]{3,2,1,0:T(8,128)}, u32[]{:S(2)}) copy-start(f32[3,8,8,128]{3,2,1,0:T(8,128)} %param.11) | copy-start | bytes 294916

commit v6 on v4

--- a/solution.py
+++ b/solution.py
@@ -556,7 +556,7 @@
     )
     ratio = pl.pallas_call(
         functools.partial(kernel, parts, columns),
-        out_shape=jax.ShapeDtypeStruct(displacement.shape, f32),
+        out_shape=pltpu.VMEM(displacement.shape, f32),
         in_specs=[pl.BlockSpec(memory_space=pltpu.HBM)] * len(operands),
         out_specs=vmem,
         scratch_shapes=[pltpu.VMEM(operand.shape, operand.dtype) for operand in operands]

time: 18 us -> 16.4 us (0.911)
  other arithmetic: 1.59 us -> 0.7 us
  Pallas kernels: 15.5 us -> 14.8 us
    add x1, other arithmetic: 1.59 us -> 0.7 us  [shards(): return (displacement + time_step * new_velocity, new_velocity)]
    pallas_call x1, Pallas kernels: 15.5 us -> 14.8 us  [shards(): pl.pallas_call(functools.partial(kernel, parts, columns), out_shape=pltpu...]
where the time goes in v6:
time: 16.4 us; the launch traced here: 16.2 us
  Pallas kernels  14.8 us (90%)
  other arithmetic  0.7 us (4%)
  between operations  0.67 us (4%)
    pallas_call x1, Pallas kernels, shards(): pl.pallas_call(functools.partial(kernel, parts, columns), out_shape=pltpu...  14.8 us
    add x1, other arithmetic, shards(): return (displacement + time_step * new_velocity, new_velocity)  0.7 us

profile of v6, /device:TPU:0, one launch (start us, length us, event | category | flops | bytes accessed | tf_op | source)
XLA Modules:
  0.0 16.2 jit_solution(9212865289629303432)
XLA Ops:
  0.6 0.0 copy-start
  0.6 0.0 copy-start.1
  0.7 14.8 %shard_map.113 = f32[3,8,8,128]{3,2,1,0:T(8,128)S(1)} custom-call(f32[3,8,8,128]{3,2,1,0:T(8,128)} %refs_0_.1, f32[8,8,128]{2,1,0:T(8,128)} %refs_1_.1, s32[1,1,16]{2,1,0:T(1,128)} %refs_2_.1, s32[1,4096]{1,0:T(1,128)} %refs_3_.1, f32[3,1,4096]{2,1,0:T(1,128)} %refs_4_.1, s32[16,1,128]{2,1,0:T(1,128)} %refs_5_.1, f32[2,16,1,128]{3,2,1,0:T(1,128)} %refs_6_.1, ...), custom_call_target="tpu_custom_call" | custom-call | tf_op jit(solution)/shard_map/pallas_call | solution.py:557
  15.5 0.0 copy-done
  15.5 0.0 copy-done.1
  15.5 0.7 %multiply_add_fusion = (f32[3,8,8,128]{3,2,1,0:T(8,128)}, f32[3,8,8,128]{3,2,1,0:T(8,128)}) fusion(f32[3,8,8,128]{3,2,1,0:T(8,128)S(1)} %copy-done, f32[3,8,8,128]{3,2,1,0:T(8,128)S(1)} %copy-done.1, f32[3,8,8,128]{3,2,1,0:T(8,128)S(1)} %shard_map.113), kind=kLoop, calls=%fused_computation | loop fusion | flops 147456 | bytes 491520 | tf_op jit(solution)/shard_map/add | solution.py:595
Async XLA Ops:
  0.6 14.9 %copy-start = (f32[3,8,8,128]{3,2,1,0:T(8,128)S(1)}, f32[3,8,8,128]{3,2,1,0:T(8,128)}, u32[]{:S(2)}) copy-start(f32[3,8,8,128]{3,2,1,0:T(8,128)} %refs_0_.1) | copy-start | bytes 294916
  0.6 14.9 %copy-start.1 = (f32[3,8,8,128]{3,2,1,0:T(8,128)S(1)}, f32[3,8,8,128]{3,2,1,0:T(8,128)}, u32[]{:S(2)}) copy-start(f32[3,8,8,128]{3,2,1,0:T(8,128)} %param.11) | copy-start | bytes 294916

commit v7 on v6

--- a/solution.py
+++ b/solution.py
@@ -173,7 +173,101 @@
     def _():
         pl.semaphore_signal(barrier, inc=1, device_id=(me, column + 1), device_id_type=MESH)
 
-    for name in ("displacement", "density", "class"):
+    for name in ("element", "coords", "displacement"):
+        copies[name].wait()
+
+    def weigh(part, carry):
+        span = pl.ds(pl.multiple_of(part * cap, lanes), cap)
+        element = element_ref[:, span]
+        along_x = quotient(element, height * depth)
+        along_y = quotient(element - along_x * (height * depth), depth)
+        along_z = element - along_x * (height * depth) - along_y * depth
+
+        def weights(lowest, along, count):
+            positions = lax.broadcasted_iota(jnp.int32, (count, cap), 0)
+            upper = jnp.where(positions == lowest + 1, along, 0.0)
+            return jnp.where(positions == lowest, 1.0 - along, upper)
+
+        weight_x[:, span] = weights(along_x, coords_ref[0, :, span], width)
+        weight_y[:, span] = weights(along_y, coords_ref[1, :, span], height)
+        high, low = halves(weights(along_z, coords_ref[2, :, span], depth))
+        weight_z[0:depth, span] = high
+        weight_z[depth : 2 * depth, span] = low
+        return carry
+
+    lax.fori_loop(0, parts, weigh, 0)
+
+    def barrier_count():
+        return (
+            parts
+            - 1
+            + jnp.where(column > 0, 1, 0)
+            + jnp.where(column < columns - 1, 1, 0)
+        )
+
+    pl.semaphore_wait(barrier, barrier_count())
+
+    def y_copy(side):
+        return pltpu.make_async_remote_copy(
+            src_ref=y_send.at[side],
+            dst_ref=y_recv.at[1 - side],
+            send_sem=y_sems.at[side],
+            recv_sem=y_sems.at[3 - side],
+            device_id=(me, column - 1 if side == 0 else column + 1),
+            device_id_type=MESH,
+        )
+
+    def x_copy(side):
+        return pltpu.make_async_remote_copy(
+            src_ref=fields.at[1 if side == 0 else width],
+            dst_ref=x_recv.at[1 - side],
+            send_sem=x_sems.at[side],
+            recv_sem=x_sems.at[3 - side],
+            device_id=(me - 1 if side == 0 else me + 1, column),
+            device_id_type=MESH,
+        )
+
+    y_there = (column > 0, column < columns - 1)
+    x_there = (me > 0, me < parts - 1)
+    def slot_copy(source, target, send_sems, recv_sems, other, slot):
+        return pltpu.make_async_remote_copy(
+            src_ref=source.at[other],
+            dst_ref=target.at[slot],
+            send_sem=send_sems.at[other],
+            recv_sem=recv_sems.at[slot],
+            device_id=(other, column),
+            device_id_type=MESH,
+        )
+
+    high, low = halves(displacement_ref[...].reshape(3 * width * height, depth))
+    count = 3 * width * height
+    both = jnp.concatenate([high, low], axis=0)
+    both = jnp.concatenate([both, both], axis=1)
+
+    def planar_weights(span):
+        planar = weight_x[:, span][:, None, :] * weight_y[:, span][None]
+        return planar.reshape(width * height, cap)
+
+    def interpolate(step, carry):
+        other = lax.rem(me + step, parts)
+        span = pl.ds(pl.multiple_of(other * cap, lanes), cap)
+        sums = dot(both, weight_z[:, span])
+        sums = sums[:count] + sums[count:]
+        planar = planar_weights(span)
+        for field in range(3):
+            piece = sums[field * width * height : (field + 1) * width * height]
+            send_out[other, field : field + 1, :] = jnp.sum(piece * planar, axis=0, keepdims=True)
+
+        @pl.when(other != me)
+        def _():
+            slot_copy(send_out, recv_out, out_send_sems, out_recv_sems, other, me).start()
+
+        return carry
+
+    lax.fori_loop(1, parts + 1, interpolate, 0)
+    recv_out[me] = send_out[me]
+
+    for name in ("density", "class"):
         copies[name].wait()
 
     block_of = quotient(lax.broadcasted_iota(jnp.int32, (1, depth), 1), block_edge)
@@ -202,105 +296,11 @@
             y_send[0, field, x : x + 1, :] = fields[x + 1, field, 0:1, :]
             y_send[1, field, x : x + 1, :] = fields[x + 1, field, height - 1 : height, :]
 
-    for name in ("element", "coords"):
-        copies[name].wait()
-
-    def weigh(part, carry):
-        span = pl.ds(pl.multiple_of(part * cap, lanes), cap)
-        element = element_ref[:, span]
-        along_x = quotient(element, height * depth)
-        along_y = quotient(element - along_x * (height * depth), depth)
-        along_z = element - along_x * (height * depth) - along_y * depth
-
-        def weights(lowest, along, count):
-            positions = lax.broadcasted_iota(jnp.int32, (count, cap), 0)
-            upper = jnp.where(positions == lowest + 1, along, 0.0)
-            return jnp.where(positions == lowest, 1.0 - along, upper)
-
-        weight_x[:, span] = weights(along_x, coords_ref[0, :, span], width)
-        weight_y[:, span] = weights(along_y, coords_ref[1, :, span], height)
-        high, low = halves(weights(along_z, coords_ref[2, :, span], depth))
-        weight_z[0:depth, span] = high
-        weight_z[depth : 2 * depth, span] = low
-        return carry
-
-    lax.fori_loop(0, parts, weigh, 0)
-
-    def barrier_count():
-        return (
-            parts
-            - 1
-            + jnp.where(column > 0, 1, 0)
-            + jnp.where(column < columns - 1, 1, 0)
-        )
-
-    pl.semaphore_wait(barrier, barrier_count())
-
-    def y_copy(side):
-        return pltpu.make_async_remote_copy(
-            src_ref=y_send.at[side],
-            dst_ref=y_recv.at[1 - side],
-            send_sem=y_sems.at[side],
-            recv_sem=y_sems.at[3 - side],
-            device_id=(me, column - 1 if side == 0 else column + 1),
-            device_id_type=MESH,
-        )
-
-    def x_copy(side):
-        return pltpu.make_async_remote_copy(
-            src_ref=fields.at[1 if side == 0 else width],
-            dst_ref=x_recv.at[1 - side],
-            send_sem=x_sems.at[side],
-            recv_sem=x_sems.at[3 - side],
-            device_id=(me - 1 if side == 0 else me + 1, column),
-            device_id_type=MESH,
-        )
-
-    y_there = (column > 0, column < columns - 1)
-    x_there = (me > 0, me < parts - 1)
     for side in range(2):
 
         @pl.when(y_there[side])
         def _():
             y_copy(side).start()
-
-    def slot_copy(source, target, send_sems, recv_sems, other, slot):
-        return pltpu.make_async_remote_copy(
-            src_ref=source.at[other],
-            dst_ref=target.at[slot],
-            send_sem=send_sems.at[other],
-            recv_sem=recv_sems.at[slot],
-            device_id=(other, column),
-            device_id_type=MESH,
-        )
-
-    high, low = halves(displacement_ref[...].reshape(3 * width * height, depth))
-    count = 3 * width * height
-    both = jnp.concatenate([high, low], axis=0)
-    both = jnp.concatenate([both, both], axis=1)
-
-    def planar_weights(span):
-        planar = weight_x[:, span][:, None, :] * weight_y[:, span][None]
-        return planar.reshape(width * height, cap)
-
-    def interpolate(step, carry):
-        other = lax.rem(me + step, parts)
-        span = pl.ds(pl.multiple_of(other * cap, lanes), cap)
-        sums = dot(both, weight_z[:, span])
-        sums = sums[:count] + sums[count:]
-        planar = planar_weights(span)
-        for field in range(3):
-            piece = sums[field * width * height : (field + 1) * width * height]
-            send_out[other, field : field + 1, :] = jnp.sum(piece * planar, axis=0, keepdims=True)
-
-        @pl.when(other != me)
-        def _():
-            slot_copy(send_out, recv_out, out_send_sems, out_recv_sems, other, me).start()
-
-        return carry
-
-    lax.fori_loop(1, parts + 1, interpolate, 0)
-    recv_out[me] = send_out[me]
 
     for name in ("slot", "angle", "stiffness", "load"):
         copies[name].wait()

time: 16.4 us -> 18.4 us (1.12)
  the two profiles are of different devices: /device:TPU:0 before, /device:TPU:1 now
where the time goes in v7:
time: 18.4 us; the launch traced here: 18.3 us
  Pallas kernels  16.9 us (92%)
  other arithmetic  0.7 us (4%)
  between operations  0.67 us (4%)
    pallas_call x1, Pallas kernels, shards(): pl.pallas_call(functools.partial(kernel, parts, columns), out_shape=pltpu...  16.9 us
    add x1, other arithmetic, shards(): return (displacement + time_step * new_velocity, new_velocity)  0.7 us

profile of v7, /device:TPU:1, one launch (start us, length us, event | category | flops | bytes accessed | tf_op | source)
XLA Modules:
  0.0 18.3 jit_solution(4496827602383346728)
XLA Ops:
  0.6 0.0 copy-start
  0.6 0.0 copy-start.1
  0.7 16.9 %shard_map.113 = f32[3,8,8,128]{3,2,1,0:T(8,128)S(1)} custom-call(f32[3,8,8,128]{3,2,1,0:T(8,128)} %refs_0_.1, f32[8,8,128]{2,1,0:T(8,128)} %refs_1_.1, s32[1,1,16]{2,1,0:T(1,128)} %refs_2_.1, s32[1,4096]{1,0:T(1,128)} %refs_3_.1, f32[3,1,4096]{2,1,0:T(1,128)} %refs_4_.1, s32[16,1,128]{2,1,0:T(1,128)} %refs_5_.1, f32[2,16,1,128]{3,2,1,0:T(1,128)} %refs_6_.1, ...), custom_call_target="tpu_custom_call" | custom-call | tf_op jit(solution)/shard_map/pallas_call | solution.py:557
  17.6 0.0 copy-done
  17.6 0.0 copy-done.1
  17.6 0.7 %multiply_add_fusion = (f32[3,8,8,128]{3,2,1,0:T(8,128)}, f32[3,8,8,128]{3,2,1,0:T(8,128)}) fusion(f32[3,8,8,128]{3,2,1,0:T(8,128)S(1)} %copy-done, f32[3,8,8,128]{3,2,1,0:T(8,128)S(1)} %copy-done.1, f32[3,8,8,128]{3,2,1,0:T(8,128)S(1)} %shard_map.113), kind=kLoop, calls=%fused_computation | loop fusion | flops 147456 | bytes 491520 | tf_op jit(solution)/shard_map/add | solution.py:595
Async XLA Ops:
  0.6 16.9 %copy-start = (f32[3,8,8,128]{3,2,1,0:T(8,128)S(1)}, f32[3,8,8,128]{3,2,1,0:T(8,128)}, u32[]{:S(2)}) copy-start(f32[3,8,8,128]{3,2,1,0:T(8,128)} %refs_0_.1) | copy-start | bytes 294916
  0.6 16.9 %copy-start.1 = (f32[3,8,8,128]{3,2,1,0:T(8,128)S(1)}, f32[3,8,8,128]{3,2,1,0:T(8,128)}, u32[]{:S(2)}) copy-start(f32[3,8,8,128]{3,2,1,0:T(8,128)} %param.11) | copy-start | bytes 294916
